TPU v7x, 32 devices: a whole 2x2x4 slice. The times are simulated.
32 devices in a mesh: grp: 4 (over y, x), docs: 8 (over z, core).
Axes of the slice: x: 2, y: 2, z: 4, core: 2. Of those that a mesh axis runs over, the one named last changes fastest.
Arguments:
- embeddings: float32 [131072, 1024], P(('grp', 'docs'))
- assign: int32 [131072], P(('grp', 'docs')), may hold values from 0 to 767, as said below
- cluster_slot: int32 [768], replicated, may hold values from 0 to 767, as said below
Outputs:
- centroids: float32 [768, 1024], P('docs')
- max_sim: float32 [131072], P(('grp', 'docs'))
- centroid_cos: float32 [131072], P(('grp', 'docs'))
Inputs may be any that keep to these rules, and one draw needn't show every extreme that they name: Each device's rows are ordered by owner, cluster_slot[assign] // 96; a device sends at most 640 rows to one owner and some device sends exactly 640; every owner receives exactly 4096 rows from the devices of its group; in each group every cluster is named by 2 to 128 rows, and some cluster by exactly 128. A permutation: cluster c is held at slot cluster_slot[c] by the owner of index cluster_slot[c] // 96 along docs.
All inputs are finite; a program needn't handle non-finite values.
Results may differ from a plain program's by a relative error of at most 0.0003.
Values may be sent and summed in bfloat16 or wider, within the bound.
No kernel may reach another device: no remote copies, remote signals or barrier semaphores. Data moves between devices by JAX's collectives and lax.ppermute only.
A program may use at most 192 MiB of HBM per device.

v0:
```python
import functools

import jax
import jax.numpy as jnp
from jax import lax
from jax.experimental import pallas as pl
from jax.experimental.pallas import tpu as pltpu
from jax.sharding import PartitionSpec as P

epsilon = 1e-06
LANES = 128
SUBLANES = 8
MIB = 1024 * 1024
TILE = 512
in_vmem = pl.BlockSpec(memory_space=pltpu.VMEM)
in_smem = pl.BlockSpec(memory_space=pltpu.SMEM)
anywhere = pl.BlockSpec(memory_space=pl.ANY)
brief = pl.CostEstimate(flops=1000, bytes_accessed=1000, transcendentals=0)


def round_up(value, step):
    return -(-value // step) * step


def params(mib=44):
    return pltpu.CompilerParams(vmem_limit_bytes=mib * MIB)


def look_up(table_ref, index):
    lane = jnp.bitwise_and(index, LANES - 1)
    row = jnp.right_shift(index, 7)
    found = jnp.zeros(index.shape, jnp.int32)
    for part in range(table_ref.shape[0]):
        entries = jnp.broadcast_to(table_ref[part : part + 1, :], index.shape)
        found = jnp.where(row == part, jnp.take_along_axis(entries, lane, axis=1), found)
    return found


def rows_below(slots, bound):
    return jnp.sum((slots < bound).astype(jnp.float32)).astype(jnp.int32)


def plan_kernel(per_owner, limit, assign_ref, table_ref, slot_ref, start_ref):
    slots = look_up(table_ref, assign_ref[...])
    slot_ref[...] = slots
    for owner in range(start_ref.shape[0]):
        start_ref[owner] = jnp.minimum(rows_below(slots, owner * per_owner), limit)


def make_plan(assign_rows, table, owner_count, per_owner, limit):
    return pl.pallas_call(
        functools.partial(plan_kernel, per_owner, limit),
        out_shape=(
            jax.ShapeDtypeStruct(assign_rows.shape, jnp.int32),
            jax.ShapeDtypeStruct((owner_count,), jnp.int32),
        ),
        in_specs=[in_vmem, in_vmem],
        out_specs=(in_vmem, in_smem),
        compiler_params=params(8),
        name="plan",
    )(assign_rows, table)


def unit_kernel(steps, offset, turn, start_ref, me_ref, rows_ref, *refs):
    unit_ref, held, sem = refs[-3:]
    part = unit_ref.shape[0] // steps
    window = part + SUBLANES
    start = start_ref[lax.rem(me_ref[0] + turn, start_ref.shape[0])] + offset

    def first(step):
        return aligned_start(start + step * part, rows_ref.shape[0], window)

    copies = [
        pltpu.make_async_copy(rows_ref.at[pl.ds(first(step), window), :], held.at[step], sem.at[step])
        for step in range(steps)
    ]
    for copy in copies:
        copy.start()
    for step in range(steps):
        copies[step].wait()
        shift = start + step * part - first(step)
        groups = held[step].reshape(window // SUBLANES, SUBLANES, -1)
        turned = pltpu.roll(groups, SUBLANES - shift, 1)
        line = lax.broadcasted_iota(jnp.int32, (part // SUBLANES, SUBLANES, groups.shape[2]), 1)
        values = jnp.where(line < SUBLANES - shift, turned[:-1], turned[1:]).reshape(part, -1)
        scale = lax.rsqrt(jnp.sum(values * values, -1, keepdims=True) + epsilon)
        unit_ref[step * part : (step + 1) * part, :] = (values * scale).astype(jnp.bfloat16)


def unit_piece(starts, me, embeddings, turn, offset, rows, after):
    width = embeddings.shape[1]
    steps = rows // LANES if rows % LANES == 0 else 1
    return pl.pallas_call(
        functools.partial(unit_kernel, steps, offset, turn),
        out_shape=jax.ShapeDtypeStruct((rows, width), jnp.bfloat16),
        in_specs=[in_smem, in_smem, anywhere] + [anywhere] * len(after),
        out_specs=in_vmem,
        scratch_shapes=[
            pltpu.VMEM((steps, rows // steps + SUBLANES, width), jnp.float32),
            pltpu.SemaphoreType.DMA((steps,)),
        ],
        compiler_params=params(),
        cost_estimate=brief,
        name="unit",
    )(starts, me, embeddings, *after)


def hold_until(values, arrived):
    def nothing(*refs):
        pass

    return pl.pallas_call(
        nothing,
        out_shape=jax.ShapeDtypeStruct(values.shape, values.dtype),
        in_specs=[anywhere] * (1 + len(arrived)),
        out_specs=anywhere,
        input_output_aliases={0: 0},
        compiler_params=params(48),
        cost_estimate=brief,
        name="hold",
    )(values, *arrived)


def aligned_start(start, row_count, window):
    begin = jnp.minimum(jnp.left_shift(jnp.right_shift(start, 3), 3), row_count - window)
    return pl.multiple_of(begin, SUBLANES)


def flat_window(held, start, rows):
    span = round_up(rows + 1, SUBLANES)
    shift = jnp.bitwise_and(start, LANES - 1)
    block = held[pl.ds(jnp.right_shift(start, 7), span), :]
    turned = pltpu.roll(block, jnp.bitwise_and(LANES - shift, LANES - 1), 1)
    following = pltpu.roll(turned, span - 1, 0)
    lane = lax.broadcasted_iota(jnp.int32, block.shape, 1)
    return jnp.where(lane < LANES - shift, turned, following)


def window_labels(held, slots, owner, start, per_owner, capacity, blocks):
    low = owner * per_owner
    mine = (slots >= low) & (slots < low + per_owner)
    held[: slots.shape[0], :] = jnp.where(mine, slots - low, -1)
    labels = flat_window(held, start, blocks)
    place = lax.broadcasted_iota(jnp.int32, labels.shape, 0) * LANES + lax.broadcasted_iota(
        jnp.int32, labels.shape, 1
    )
    return jnp.where(place < capacity, labels, -1)


def summed_kernel(per_owner, capacity, start_ref, slot_ref, sum_ref, held):
    owner_count = sum_ref.shape[0]
    held[...] = jnp.full(held.shape, -1, jnp.int32)
    slots = slot_ref[...]
    window = capacity + SUBLANES
    wide = sum_ref.shape[1] // LANES
    for owner in range(owner_count):
        aligned = aligned_start(start_ref[owner], slots.size, window)
        labels = window_labels(held, slots, owner, aligned, per_owner, window, wide)
        for block in range(wide):
            sum_ref[owner : owner + 1, block * LANES : (block + 1) * LANES] = labels[block : block + 1, :]


def summed_labels(starts, slots, owner_count, per_owner, capacity):
    return pl.pallas_call(
        functools.partial(summed_kernel, per_owner, capacity),
        out_shape=jax.ShapeDtypeStruct((owner_count, round_up(capacity + SUBLANES, LANES)), jnp.int32),
        in_specs=[in_smem, in_vmem],
        out_specs=in_vmem,
        scratch_shapes=[pltpu.VMEM((slots.shape[0] + 2 * SUBLANES, LANES), jnp.int32)],
        compiler_params=params(8),
        name="summed",
    )(starts, slots)


def sent_kernel(per_owner, capacity, start_ref, slot_ref, after_ref, sent_ref, held):
    owner_count, span, _ = sent_ref.shape
    held[...] = jnp.full(held.shape, -1, jnp.int32)
    slots = slot_ref[...]
    for owner in range(owner_count):
        labels = window_labels(held, slots, owner, start_ref[owner], per_owner, capacity, span - 1)
        sent_ref[owner] = labels[:span, :]


def sent_labels(starts, slots, owner_count, per_owner, capacity, after):
    span = round_up(-(-capacity // LANES) + 1, SUBLANES)
    return pl.pallas_call(
        functools.partial(sent_kernel, per_owner, capacity),
        out_shape=jax.ShapeDtypeStruct((owner_count, span, LANES), jnp.int32),
        in_specs=[in_smem, in_vmem, anywhere],
        out_specs=in_vmem,
        scratch_shapes=[pltpu.VMEM((slots.shape[0] + 2 * SUBLANES, LANES), jnp.int32)],
        compiler_params=params(8),
        name="sent",
    )(starts, slots, after)


def arrived_kernel(blocks, turns_of, me_ref, got_ref, row_ref, column_ref, tally_ref):
    tally = jnp.zeros((LANES, LANES), jnp.float32)
    cluster = lax.broadcasted_iota(jnp.int32, tally.shape, 0)
    for place, turn in enumerate(turns_of):
        source = lax.rem(me_ref[0] + len(turns_of) - turn, len(turns_of))
        for block in range(blocks):
            line = place * blocks + block
            spread = jnp.broadcast_to(got_ref[source, block : block + 1, :], tally.shape)
            row_ref[line : line + 1, :] = spread[:1, :]
            column_ref[line * LANES : (line + 1) * LANES, :] = spread.T
            tally += (spread == cluster).astype(jnp.float32)
    total = jnp.broadcast_to(jnp.sum(tally, 1, keepdims=True), tally.shape)
    tally_ref[...] = jnp.zeros(tally_ref.shape, jnp.float32)
    tally_ref[:, :LANES] = total.T[:SUBLANES, :]


def arrived_labels(me, got, turns_of, blocks, width):
    lines = len(turns_of) * blocks
    return pl.pallas_call(
        functools.partial(arrived_kernel, blocks, turns_of),
        out_shape=(
            jax.ShapeDtypeStruct((lines, LANES), jnp.int32),
            jax.ShapeDtypeStruct((lines * LANES, LANES), jnp.int32),
            jax.ShapeDtypeStruct((SUBLANES, width), jnp.float32),
        ),
        in_specs=[in_smem, in_vmem],
        out_specs=(in_vmem, in_vmem, in_vmem),
        compiler_params=params(8),
        name="arrived",
    )(me, got)


def sum_kernel(start_ref, label_ref, rows_ref, *refs):
    sum_ref, held, sem = refs[-3:]
    owner_count, per_owner, _ = sum_ref.shape
    window = held.shape[1]

    def copy(owner, slot):
        first = aligned_start(start_ref[owner], rows_ref.shape[0], window)
        return pltpu.make_async_copy(rows_ref.at[pl.ds(first, window), :], held.at[slot], sem.at[slot])

    copy(0, 0).start()

    def body(owner, carry):
        slot = lax.rem(owner, 2)

        @pl.when(owner + 1 < owner_count)
        def _():
            copy(owner + 1, 1 - slot).start()

        copy(owner, slot).wait()
        labels = label_ref[pl.ds(owner, 1), :][:, :window]
        cluster = lax.broadcasted_iota(jnp.int32, (per_owner, window), 0)
        member = (labels == cluster).astype(jnp.float32).astype(jnp.bfloat16)
        values = held[slot]
        high = values.astype(jnp.bfloat16)
        rest = values - high.astype(jnp.float32)
        middle = rest.astype(jnp.bfloat16)
        low = (rest - middle.astype(jnp.float32)).astype(jnp.bfloat16)
        total = jnp.dot(member, high, preferred_element_type=jnp.float32)
        total += jnp.dot(member, middle, preferred_element_type=jnp.float32)
        total += jnp.dot(member, low, preferred_element_type=jnp.float32)
        sum_ref[pl.ds(owner, 1)] = total[None]
        return carry

    lax.fori_loop(0, owner_count, body, 0)


def slot_sums(starts, labels, embeddings, per_owner, capacity, after):
    owner_count = labels.shape[0]
    width = embeddings.shape[1]
    return pl.pallas_call(
        sum_kernel,
        out_shape=jax.ShapeDtypeStruct((owner_count, per_owner, width), jnp.float32),
        in_specs=[in_smem, in_vmem, anywhere] + [anywhere] * len(after),
        out_specs=in_vmem,
        scratch_shapes=[
            pltpu.VMEM((2, capacity + SUBLANES, width), jnp.float32),
            pltpu.SemaphoreType.DMA((2,)),
        ],
        compiler_params=params(),
        cost_estimate=pl.CostEstimate(
            flops=6 * owner_count * per_owner * capacity * width,
            bytes_accessed=4 * embeddings.size,
            transcendentals=0,
        ),
        name="sums",
    )(starts, labels, embeddings, *after)


def gram_kernel(begin, rows, wide, after_count, turns_of, *refs):
    chunk_ref, row_ref, column_ref, best_ref, *refs = refs
    flat_ref = centroid_ref = result_ref = None
    if begin:
        flat_ref, *refs = refs
    refs = refs[after_count:]
    if turns_of:
        centroid_ref, me_ref, result_ref, *refs, out_ref, cosine_ref = refs
    else:
        out_ref, flat_ref, *refs = refs
    mine, turned, labels, tiles, even, odd, best, sem, tile_sem = refs
    first = begin // LANES
    size = tiles.shape[2]
    count = -(-begin // size)

    def line_of(tile):
        return jnp.minimum(tile * (size // LANES), first - size // LANES)

    def fetch(tile):
        start = pl.multiple_of(line_of(tile) * LANES, LANES)
        slot = lax.rem(tile, 4)
        return pltpu.make_async_copy(flat_ref.at[:, pl.ds(start, size)], tiles.at[slot], tile_sem.at[slot])

    chunk_copy = pltpu.make_async_copy(chunk_ref, mine.at[pl.ds(0, rows), :], sem.at[0])
    label_copy = pltpu.make_async_copy(column_ref.at[pl.ds(begin, wide), :], labels, sem.at[1])
    chunk_copy.start()
    label_copy.start()
    for tile in range(min(count, 3)):
        fetch(jnp.int32(tile)).start()
    if rows < wide:
        mine[rows:wide, :] = jnp.zeros((wide - rows, mine.shape[1]), mine.dtype)
    if turns_of:
        mine[wide:, :] = centroid_ref[...]
        cosine_ref[...] = jnp.zeros(cosine_ref.shape, jnp.float32)
    out_ref[...] = best_ref[...]
    best[...] = jnp.full(best.shape, -2.0, jnp.float32)
    chunk_copy.wait()
    label_copy.wait()
    turned[...] = mine[:wide, :].T
    if not turns_of:
        flat_copy = pltpu.make_async_copy(turned, flat_ref.at[:, pl.ds(begin, wide)], sem.at[2])
        flat_copy.start()

    def products(right):
        return jnp.dot(mine[...], right, preferred_element_type=jnp.float32)

    halves = 2 if size % (4 * LANES) == 0 else 1

    def multiply(held, slot, half):
        here = slice(half * (size // halves), (half + 1) * (size // halves))
        held[:, here] = products(tiles[slot, :, here])

    def cosines(values, line):
        cluster = lax.broadcasted_iota(jnp.int32, values.shape, 0)
        own = jnp.where(row_ref[pl.ds(line, 1), :] == cluster, values, 0.0)
        cosine_ref[pl.ds(line, 1), :] = jnp.sum(own, 0, keepdims=True)

    def reduce_tile(held, tile, half):
        parts = range(half * (size // halves) // LANES, (half + 1) * (size // halves) // LANES)
        lines = {part: line_of(tile) + part for part in parts}
        tops = {part: jnp.full((SUBLANES, LANES), -2.0, jnp.float32) for part in parts}
        against = {
            part: jnp.broadcast_to(row_ref[pl.ds(lines[part], 1), :], (LANES, LANES)) for part in parts
        }
        for begin_row in range(0, wide, LANES):
            span = slice(begin_row, begin_row + LANES)
            own = labels[span, :]
            fold = best[span, :]
            for part in parts:
                near = jnp.where(own == against[part], held[span, part * LANES : (part + 1) * LANES], -2.0)
                fold = jnp.maximum(fold, near)
                tops[part] = jnp.maximum(tops[part], jnp.max(near.reshape(-1, SUBLANES, LANES), 0))
            best[span, :] = fold
        for part in parts:
            out_ref[pl.ds(lines[part], 1), :] = jnp.maximum(
                out_ref[pl.ds(lines[part], 1), :], jnp.max(tops[part], 0, keepdims=True)
            )
            if turns_of:
                cosines(held[wide:, part * LANES : (part + 1) * LANES], lines[part])

    if begin:
        fetch(jnp.int32(0)).wait()
        for half in range(halves):
            multiply(even, 0, half)

        def body(pair, carry):
            tile = pair * 2
            fetch(tile + 1).wait()

            @pl.when(tile + 3 < count)
            def _():
                fetch(tile + 3).start()

            for half in range(halves):
                multiply(odd, lax.rem(tile + 1, 4), half)
                reduce_tile(even, tile, half)
            fetch(tile + 2).wait()

            @pl.when(tile + 4 < count)
            def _():
                fetch(tile + 4).start()

            for half in range(halves):
                multiply(even, lax.rem(tile + 2, 4), half)
                reduce_tile(odd, tile + 1, half)
            return carry

        lax.fori_loop(0, (count - 1) // 2, body, 0)
        left = even
        if count % 2 == 0:
            left = odd
            fetch(jnp.int32(count - 1)).wait()
            for half in range(halves):
                multiply(odd, (count - 1) % 4, half)
                reduce_tile(even, jnp.int32(count - 2), half)
        for half in range(halves):
            reduce_tile(left, jnp.int32(count - 1), half)
    own = products(turned[...])
    row = lax.broadcasted_iota(jnp.int32, (wide, LANES), 0)
    column = lax.broadcasted_iota(jnp.int32, (wide, LANES), 1)
    for block in range(wide // LANES):
        line = first + block
        here = slice(block * LANES, (block + 1) * LANES)
        allowed = (labels[...] == row_ref[line : line + 1, :]) & (row != column + block * LANES)
        near = jnp.max(jnp.where(allowed, own[:wide, here], -2.0), 0, keepdims=True)
        other = jnp.max(best[here, :].T, 0, keepdims=True)
        out_ref[line : line + 1, :] = jnp.maximum(near, other)
        if turns_of:
            cosines(own[wide:, here], line)
    if turns_of:
        blocks = row_ref.shape[0] // len(turns_of)
        half = result_ref.shape[1] // 2
        result_ref[...] = jnp.zeros(result_ref.shape, jnp.float32)
        for place, turn in enumerate(turns_of):
            source = lax.rem(me_ref[0] + len(turns_of) - turn, len(turns_of))
            lines = slice(place * blocks, (place + 1) * blocks)
            result_ref[source, :blocks, :] = out_ref[lines, :]
            result_ref[source, half : half + blocks, :] = cosine_ref[lines, :]
    else:
        flat_copy.wait()


def gram_step(rows, columns, best, flat, chunk, begin, after=(), final=None):
    length, width = chunk.shape
    wide = round_up(length, LANES)
    tall = wide
    size = min(TILE, begin) if begin else LANES
    flat_shape = jax.ShapeDtypeStruct((width, columns.shape[0]), jnp.bfloat16)
    inputs = [chunk, rows, columns, best]
    in_specs = [anywhere, in_vmem, anywhere, in_vmem]
    aliases = {}
    if begin:
        if not final:
            aliases = {len(inputs): 1}
        inputs.append(flat)
        in_specs.append(anywhere)
    inputs += after
    in_specs += [anywhere] * len(after)
    out_shape = (jax.ShapeDtypeStruct(best.shape, jnp.float32), flat_shape)
    out_specs = (in_vmem, anywhere)
    turns_of = ()
    extra = []
    if final:
        centroid_unit, me, turns_of = final
        tall += centroid_unit.shape[0]
        inputs += [centroid_unit, me]
        in_specs += [in_vmem, in_smem]
        half = round_up(rows.shape[0] // len(turns_of) + 1, SUBLANES)
        out_shape = jax.ShapeDtypeStruct((len(turns_of), 2 * half, LANES), jnp.float32)
        out_specs = in_vmem
        extra = [pltpu.VMEM(best.shape, jnp.float32)] * 2
    return pl.pallas_call(
        functools.partial(gram_kernel, begin, length, wide, len(after), turns_of),
        out_shape=out_shape,
        in_specs=in_specs,
        out_specs=out_specs,
        scratch_shapes=[
            pltpu.VMEM((tall, width), jnp.bfloat16),
            pltpu.VMEM((width, wide), jnp.bfloat16),
            pltpu.VMEM((wide, LANES), jnp.int32),
            pltpu.VMEM((4, width, size), jnp.bfloat16),
            pltpu.VMEM((tall, size), jnp.float32),
            pltpu.VMEM((tall, size), jnp.float32),
            pltpu.VMEM((wide, LANES), jnp.float32),
            pltpu.SemaphoreType.DMA((3,)),
            pltpu.SemaphoreType.DMA((4,)),
        ]
        + extra,
        input_output_aliases=aliases,
        compiler_params=params(),
        cost_estimate=brief,
        name="gram",
    )(*inputs)


def pack_kernel(share_ref, tally_ref, *refs):
    packed_ref = refs[-1]
    packed_ref[: share_ref.shape[0], :] = share_ref[...]
    packed_ref[share_ref.shape[0] :, :] = tally_ref[...]


def pack_share(share, tally, after):
    length = share.shape[0] + tally.shape[0]
    return pl.pallas_call(
        pack_kernel,
        out_shape=jax.ShapeDtypeStruct((length, share.shape[1]), jnp.float32),
        in_specs=[in_vmem, in_vmem] + [anywhere] * len(after),
        out_specs=in_vmem,
        compiler_params=params(8),
        name="pack",
    )(share, tally, *after)


def centroid_kernel(gathered_ref, centroid_ref, unit_ref):
    groups, length, width = gathered_ref.shape
    share = length - SUBLANES
    per_owner = centroid_ref.shape[0]
    tally = jnp.sum(gathered_ref[:, share, :LANES], 0, keepdims=True)
    column = jnp.broadcast_to(tally, (LANES, LANES)).T[:per_owner, :]
    sums = jnp.concatenate([gathered_ref[group, :share, :] for group in range(groups)], 0)
    centroids = sums / jnp.concatenate([column] * (width // LANES), 1)
    centroid_ref[...] = centroids
    scale = lax.rsqrt(jnp.sum(centroids * centroids, -1, keepdims=True) + epsilon)
    unit_ref[...] = (centroids * scale).astype(jnp.bfloat16)


def make_centroids(gathered, per_owner):
    shape = (per_owner, gathered.shape[2])
    return pl.pallas_call(
        centroid_kernel,
        out_shape=(
            jax.ShapeDtypeStruct(shape, jnp.float32),
            jax.ShapeDtypeStruct(shape, jnp.bfloat16),
        ),
        in_specs=[in_vmem],
        out_specs=(in_vmem, in_vmem),
        compiler_params=params(8),
        name="centroids",
    )(gathered)


def place_kernel(per_owner, start_ref, slot_ref, back_ref, near_ref, cosine_ref, held, result):
    owner_count, double, _ = back_ref.shape
    span = double // 2
    rows = slot_ref.shape[0]
    held[...] = jnp.full(held.shape, -1, jnp.int32)
    held[:rows, :] = slot_ref[...]
    result[...] = jnp.zeros(result.shape, jnp.float32)
    lane = lax.broadcasted_iota(jnp.int32, (span, LANES), 1)
    for owner in range(owner_count):
        start = start_ref[owner]
        first = pl.ds(jnp.right_shift(start, 7), span)
        shift = jnp.bitwise_and(start, LANES - 1)
        slots = held[first, :]
        mine = (slots >= owner * per_owner) & (slots < (owner + 1) * per_owner)
        for kind in range(2):
            turned = pltpu.roll(back_ref[owner, kind * span : (kind + 1) * span, :], shift, 1)
            earlier = pltpu.roll(turned, 1, 0)
            moved = jnp.where(lane >= shift, turned, earlier)
            result[kind, first, :] = jnp.where(mine, moved, result[kind, first, :])
    near_ref[...] = result[0, :rows, :]
    cosine_ref[...] = result[1, :rows, :]


def place_rows(starts, slots, back, per_owner):
    span = back.shape[1] // 2
    rows = slots.shape[0]
    return pl.pallas_call(
        functools.partial(place_kernel, per_owner),
        out_shape=(jax.ShapeDtypeStruct(slots.shape, jnp.float32),) * 2,
        in_specs=[in_smem, in_vmem, in_vmem],
        out_specs=(in_vmem, in_vmem),
        scratch_shapes=[
            pltpu.VMEM((rows + span, LANES), jnp.int32),
            pltpu.VMEM((2, rows + span, LANES), jnp.float32),
        ],
        compiler_params=params(8),
        name="place",
    )(starts, slots, back)


def turns(count):
    order = sorted(range(count), key=lambda turn: (min(turn, count - turn), turn))
    if count == 8:
        order = [0, 1, 2, 3, 7, 6, 5, 4]
    return order


def per_device(embeddings, assign, cluster_slot):
    row_count, width = embeddings.shape
    owner_count = lax.axis_size("docs")
    per_owner = cluster_slot.shape[0] // owner_count
    capacity = row_count // owner_count + row_count // (4 * owner_count)
    padded = round_up(capacity, LANES)
    blocks = padded // LANES
    me = lax.axis_index("docs").astype(jnp.int32).reshape(1)
    turns_of = turns(owner_count)

    slots, starts = make_plan(
        assign.reshape(-1, LANES), cluster_slot.reshape(-1, LANES), owner_count, per_owner, row_count - capacity
    )

    sent = []
    for place, turn in enumerate(turns_of):
        sent.append(unit_piece(starts, me, embeddings, turn, 0, capacity, sent[-1:] if place > 1 else []))

    def travel(place, piece):
        turn = turns_of[place]
        return lax.ppermute(piece, "docs", [(i, (i + turn) % owner_count) for i in range(owner_count)])

    chunks = [sent[0]] + [travel(place, sent[place]) for place in (1, 2, 3)]
    sum_labels = summed_labels(starts, slots, owner_count, per_owner, capacity)
    partial_sums = slot_sums(starts, sum_labels, embeddings, per_owner, capacity, sent[1:8])
    partial_sums = hold_until(partial_sums, chunks[1:3])
    wire_labels = sent_labels(starts, slots, owner_count, per_owner, capacity, partial_sums)
    got_labels = lax.all_to_all(wire_labels, "docs", split_axis=0, concat_axis=0, tiled=True)
    rows, columns, group_tally = arrived_labels(me, got_labels, turns_of, blocks, width)
    group_share = lax.psum_scatter(partial_sums, "grp", scatter_dimension=1, tiled=True)
    group_share = hold_until(group_share, [chunks[3], got_labels])
    share = lax.psum_scatter(group_share, "docs", scatter_dimension=0, tiled=True)[0]
    for place in range(4, owner_count):
        after = [chunks[4]] if place == owner_count - 1 else [chunks[3], got_labels]
        chunks.append(travel(place, hold_until(sent[place], after)))

    bests = [jnp.full((owner_count * blocks, LANES), -2.0, jnp.float32)]
    flat = None
    for place in range(owner_count - 1):
        after = []
        if place == owner_count - 2:
            packed = pack_share(share, group_tally, bests[-2:-1])
            centroids, centroid_unit = make_centroids(lax.all_gather(packed, "grp"), per_owner)
            after = [centroid_unit]
        best, flat = gram_step(rows, columns, bests[-1], flat, chunks[place], place * padded, after)
        bests.append(best)
    results = gram_step(
        rows, columns, bests[-1], flat, chunks[-1], (owner_count - 1) * padded, final=(centroid_unit, me, turns_of)
    )
    back = lax.all_to_all(results, "docs", split_axis=0, concat_axis=0, tiled=True)
    near, cosine = place_rows(starts, slots, back, per_owner)
    return (centroids, near.reshape(-1), cosine.reshape(-1))


def solution(mesh):
    placed = (P(("grp", "docs"), None), P(("grp", "docs")), P())
    return jax.shard_map(
        per_device,
        mesh=mesh,
        in_specs=placed,
        out_specs=(P("docs", None), P(("grp", "docs")), P(("grp", "docs"))),
        check_vma=False,
    )
```

profile of v0, /device:TPU:0, one launch (start us, length us, event | category | flops | bytes accessed | tf_op | source)
XLA Modules:
  0.0 296.6 jit_solution(10709677299876037435)
XLA Ops:
  9.5 2.5 unit.8.refs_0_
  12.0 2.5 unit.9.refs_0_.refs_1_
  14.5 3.1 %collective-permute-start.1 = (bf16[640,1024]{1,0:T(8,128)(2,1)S(1)}, bf16[640,1024]{1,0:T(8,128)(2,1)S(1)}, u32[]{:S(2)}, u32[]{:S(2)}) collective-permute-start(bf16[640,1024]{1,0:T(8,128)(2,1)S(1)} %unit.9.refs_0_.refs_1_), channel_id=1, source_target_pairs={{0,2},{1,3},{2,4},{3,5},{4,6},{5,7},{6,0},{7,1},{8,10},{9,11},{10,... | collective-permute-start | bytes 3932168 | tf_op jit(solution)/shard_map/ppermute | solution.py:595
  20.0 3.6 %unit.11.refs_0_.refs_3_ = bf16[640,1024]{1,0:T(8,128)(2,1)} custom-call(s32[8]{0:T(128)S(1)} %get-tuple-element.26.start_ref, s32[1]{0:T(128)} %bitcast.2.me_ref.refs_6_, f32[4096,1024]{1,0:T(8,128)} %rows_ref.17, bf16[640,1024]{1,0:T(8,128)(2,1)S(1)} %unit.10.refs_0_.refs_2_), custom_call_target="tpu_custom_call" | custom-call | flops 1000 | bytes 1000 | tf_op jit(solution)/shard_map/unit/pallas_call | solution.py:93
  23.6 3.6 %unit.12.refs_0_.refs_4_ = bf16[640,1024]{1,0:T(8,128)(2,1)} custom-call(s32[8]{0:T(128)S(1)} %get-tuple-element.26.start_ref, s32[1]{0:T(128)} %bitcast.2.me_ref.refs_6_, f32[4096,1024]{1,0:T(8,128)} %rows_ref.17, bf16[640,1024]{1,0:T(8,128)(2,1)} %unit.11.refs_0_.refs_3_), custom_call_target="tpu_custom_call" | custom-call | flops 1000 | bytes 1000 | tf_op jit(solution)/shard_map/unit/pallas_call | solution.py:93
  27.2 3.5 %unit.13.refs_0_.refs_5_ = bf16[640,1024]{1,0:T(8,128)(2,1)} custom-call(s32[8]{0:T(128)S(1)} %get-tuple-element.26.start_ref, s32[1]{0:T(128)} %bitcast.2.me_ref.refs_6_, f32[4096,1024]{1,0:T(8,128)} %rows_ref.17, bf16[640,1024]{1,0:T(8,128)(2,1)} %unit.12.refs_0_.refs_4_), custom_call_target="tpu_custom_call" | custom-call | flops 1000 | bytes 1000 | tf_op jit(solution)/shard_map/unit/pallas_call | solution.py:93
  30.7 3.5 %unit.14.refs_6_.refs_0_ = bf16[640,1024]{1,0:T(8,128)(2,1)} custom-call(s32[8]{0:T(128)S(1)} %get-tuple-element.26.start_ref, s32[1]{0:T(128)} %bitcast.2.me_ref.refs_6_, f32[4096,1024]{1,0:T(8,128)} %rows_ref.17, bf16[640,1024]{1,0:T(8,128)(2,1)} %unit.13.refs_0_.refs_5_), custom_call_target="tpu_custom_call" | custom-call | flops 1000 | bytes 1000 | tf_op jit(solution)/shard_map/unit/pallas_call | solution.py:93
  34.9 14.9 %sums.1.refs_0_ = f32[8,96,1024]{2,1,0:T(8,128)} custom-call(s32[8]{0:T(128)S(1)} %get-tuple-element.26.start_ref, s32[8,768]{1,0:T(8,128)S(1)} %summed.1.label_ref, f32[4096,1024]{1,0:T(8,128)} %rows_ref.17, bf16[640,1024]{1,0:T(8,128)(2,1)S(1)} %unit.8.refs_0_, bf16[640,1024]{1,0:T(8,128)(2,1)S(1)} %unit.9.refs_0_.refs_1_, ...), custom_call_target="tpu_custom_call" | custom-call | flops 3019898880 | bytes 16777216 | tf_op jit(solution)/shard_map/sums/pallas_call | solution.py:268
  49.9 12.5 %collective-permute-done.refs_1_.refs_0_ = bf16[640,1024]{1,0:T(8,128)(2,1)S(1)} collective-permute-done((bf16[640,1024]{1,0:T(8,128)(2,1)S(1)}, bf16[640,1024]{1,0:T(8,128)(2,1)S(1)}, u32[]{:S(2)}, u32[]{:S(2)}) %collective-permute-start) | collective-permute-done | bytes 1310752 | tf_op jit(solution)/shard_map/ppermute | solution.py:595
  71.2 3.3 %all-to-all-start = ((s32[8,8,128]{2,1,0:T(8,128)}), s32[8,8,128]{2,1,0:T(8,128)S(1)}, u32[]{:S(2)}, u32[]{:S(2)}) async-start(s32[8,8,128]{2,1,0:T(8,128)} %sent.1), calls=%async_computation.1 | async-start | bytes 65536 | tf_op jit(solution)/shard_map/all_to_all | solution.py:602
  74.6 39.5 %collective-permute-done.2.refs_1_.refs_0_ = bf16[640,1024]{1,0:T(8,128)(2,1)} collective-permute-done((bf16[640,1024]{1,0:T(8,128)(2,1)}, bf16[640,1024]{1,0:T(8,128)(2,1)}, u32[]{:S(2)}, u32[]{:S(2)}) %collective-permute-start.2) | collective-permute-done | bytes 1310752 | tf_op jit(solution)/shard_map/ppermute | solution.py:595
  118.2 30.2 %collective-permute-done.3.refs_0_.refs_1_ = bf16[640,1024]{1,0:T(8,128)(2,1)S(1)} collective-permute-done((bf16[640,1024]{1,0:T(8,128)(2,1)}, bf16[640,1024]{1,0:T(8,128)(2,1)S(1)}, u32[]{:S(2)}, u32[]{:S(2)}) %collective-permute-start.3) | collective-permute-done | bytes 1310752 | tf_op jit(solution)/shard_map/ppermute | solution.py:595
  153.0 2.5 gram.8
  155.5 5.1 %gram.9 = (f32[40,128]{1,0:T(8,128)S(1)}, bf16[1024,5120]{1,0:T(8,128)(2,1)}) custom-call(bf16[640,1024]{1,0:T(8,128)(2,1)S(1)} %copy-done.7, s32[40,128]{1,0:T(8,128)S(1)} %get-tuple-element.29.refs_1_, s32[5120,128]{1,0:T(8,128)S(1)} %get-tuple-element.30.refs_2_, f32[40,128]{1,0:T(8,128)S(1)} %get-tuple-element.31.refs_3_, ...), custom_call_target="tpu_custom_call", output_to_operand_aliasing={{1}: (4, {})} | custom-call | flops 1000 | bytes 1000 | tf_op jit(solution)/shard_map/gram/pallas_call | solution.py:458
  160.7 6.0 %gram.10 = (f32[40,128]{1,0:T(8,128)S(1)}, bf16[1024,5120]{1,0:T(8,128)(2,1)}) custom-call(bf16[640,1024]{1,0:T(8,128)(2,1)S(1)} %copy-done.5, s32[40,128]{1,0:T(8,128)S(1)} %get-tuple-element.29.refs_1_, s32[5120,128]{1,0:T(8,128)S(1)} %get-tuple-element.30.refs_2_, f32[40,128]{1,0:T(8,128)S(1)} %get-tuple-element.33.refs_3_, ...), custom_call_target="tpu_custom_call", output_to_operand_aliasing={{1}: (4, {})} | custom-call | flops 1000 | bytes 1000 | tf_op jit(solution)/shard_map/gram/pallas_call | solution.py:458
  166.7 7.4 %gram.11 = (f32[40,128]{1,0:T(8,128)S(1)}, bf16[1024,5120]{1,0:T(8,128)(2,1)}) custom-call(bf16[640,1024]{1,0:T(8,128)(2,1)} %collective-permute-done.2.refs_1_.refs_0_, s32[40,128]{1,0:T(8,128)S(1)} %get-tuple-element.29.refs_1_, s32[5120,128]{1,0:T(8,128)S(1)} %get-tuple-element.30.refs_2_, ...), custom_call_target="tpu_custom_call", output_to_operand_aliasing={{1}: (4, {})} | custom-call | flops 1000 | bytes 1000 | tf_op jit(solution)/shard_map/gram/pallas_call | solution.py:458
  174.1 7.8 %gram.12 = (f32[40,128]{1,0:T(8,128)S(1)}, bf16[1024,5120]{1,0:T(8,128)(2,1)}) custom-call(bf16[640,1024]{1,0:T(8,128)(2,1)S(1)} %copy-done.9, s32[40,128]{1,0:T(8,128)S(1)} %get-tuple-element.29.refs_1_, s32[5120,128]{1,0:T(8,128)S(1)} %get-tuple-element.30.refs_2_, f32[40,128]{1,0:T(8,128)S(1)} %get-tuple-element.37.refs_3_, ...), custom_call_target="tpu_custom_call", output_to_operand_aliasing={{1}: (4, {})} | custom-call | flops 1000 | bytes 1000 | tf_op jit(solution)/shard_map/gram/pallas_call | solution.py:458
  181.9 9.5 %gram.13 = (f32[40,128]{1,0:T(8,128)S(1)}, bf16[1024,5120]{1,0:T(8,128)(2,1)}) custom-call(bf16[640,1024]{1,0:T(8,128)(2,1)S(1)} %collective-permute-done.6.refs_0_, s32[40,128]{1,0:T(8,128)S(1)} %get-tuple-element.29.refs_1_, s32[5120,128]{1,0:T(8,128)S(1)} %get-tuple-element.30.refs_2_, ...), custom_call_target="tpu_custom_call", output_to_operand_aliasing={{1}: (4, {})} | custom-call | flops 1000 | bytes 1000 | tf_op jit(solution)/shard_map/gram/pallas_call | solution.py:458
  191.4 38.0 %reduce-scatter.5.cloned.1.call-done = f32[1,24,1024]{2,1,0:T(8,128)} async-done(((f32[8,24,1024]{2,1,0:T(8,128)}), f32[1,24,1024]{2,1,0:T(8,128)}) %reduce-scatter.5.cloned.1.call-update) | async-done | bytes 98320 | tf_op jit(solution)/shard_map/reduce_scatter | solution.py:606
  230.3 10.3 %all-gather = f32[128,1024]{1,0:T(8,128)S(1)} all-gather(f32[32,1024]{1,0:T(8,128)S(1)} %pack.1), channel_id=2, replica_groups=mesh['grp'=4,'docs'=8] {'grp'}, dimensions={0}, use_global_device_ids=true | all-gather | bytes 655360 | tf_op jit(solution)/shard_map/all_gather | solution.py:617
  241.5 10.6 %gram.14 = (f32[40,128]{1,0:T(8,128)S(1)}, bf16[1024,5120]{1,0:T(8,128)(2,1)}) custom-call(bf16[640,1024]{1,0:T(8,128)(2,1)} %collective-permute-done.5.refs_0_, s32[40,128]{1,0:T(8,128)S(1)} %get-tuple-element.29.refs_1_, s32[5120,128]{1,0:T(8,128)S(1)} %get-tuple-element.30.refs_2_, ...), custom_call_target="tpu_custom_call", output_to_operand_aliasing={{1}: (4, {})} | custom-call | flops 1000 | bytes 1000 | tf_op jit(solution)/shard_map/gram/pallas_call | solution.py:458
  252.1 13.2 %collective-permute-done.4.refs_0_ = bf16[640,1024]{1,0:T(8,128)(2,1)} collective-permute-done((bf16[640,1024]{1,0:T(8,128)(2,1)}, bf16[640,1024]{1,0:T(8,128)(2,1)}, u32[]{:S(2)}, u32[]{:S(2)}) %collective-permute-start.4) | collective-permute-done | bytes 1310752 | tf_op jit(solution)/shard_map/ppermute | solution.py:595
  265.2 13.1 %gram.15 = f32[8,16,128]{2,1,0:T(8,128)S(1)} custom-call(bf16[640,1024]{1,0:T(8,128)(2,1)} %collective-permute-done.4.refs_0_, s32[40,128]{1,0:T(8,128)S(1)} %get-tuple-element.29.refs_1_, s32[5120,128]{1,0:T(8,128)S(1)} %get-tuple-element.30.refs_2_, f32[40,128]{1,0:T(8,128)S(1)} %get-tuple-element.45.refs_3_, ...), custom_call_target="tpu_custom_call" | custom-call | flops 1000 | bytes 1000 | tf_op jit(solution)/shard_map/gram/pallas_call | solution.py:458
  278.4 10.1 %all_to_all.10.back_ref = f32[8,16,128]{2,1,0:T(8,128)S(1)} all-to-all(f32[8,16,128]{2,1,0:T(8,128)S(1)} %gram.15), channel_id=1, replica_groups=mesh['grp'=4,'docs'=8] {'docs'}, dimensions={0} | all-to-all | bytes 131072 | tf_op jit(solution)/shard_map/all_to_all | solution.py:624
  (61 shorter events, 25.9 us)
Async XLA Ops:
  7.2 107.7 %reduce-scatter.3.cloned.1.call-start = ((), (), s32[]{:S(2)}) async-start(), calls=%async_computation.4 | async-start | bytes 3932160 | tf_op jit(solution)/shard_map/reduce_scatter | solution.py:604
  7.2 0.7 copy-start.13
  14.5 35.4 %collective-permute-start.1 = (bf16[640,1024]{1,0:T(8,128)(2,1)S(1)}, bf16[640,1024]{1,0:T(8,128)(2,1)S(1)}, u32[]{:S(2)}, u32[]{:S(2)}) collective-permute-start(bf16[640,1024]{1,0:T(8,128)(2,1)S(1)} %unit.9.refs_0_.refs_1_), channel_id=1, source_target_pairs={{0,2},{1,3},{2,4},{3,5},{4,6},{5,7},{6,0},{7,1},{8,10},{9,11},{10,... | collective-permute-start | bytes 3932168 | tf_op jit(solution)/shard_map/ppermute | solution.py:595
  17.5 44.8 %collective-permute-start = (bf16[640,1024]{1,0:T(8,128)(2,1)S(1)}, bf16[640,1024]{1,0:T(8,128)(2,1)S(1)}, u32[]{:S(2)}, u32[]{:S(2)}) collective-permute-start(bf16[640,1024]{1,0:T(8,128)(2,1)S(1)} %unit.8.refs_0_), channel_id=1, source_target_pairs={{0,1},{1,2},{2,3},{3,4},{4,5},{5,6},{6,7},{7,0},{8,9},{9,10},{10,1... | collective-permute-start | bytes 3932168 | tf_op jit(solution)/shard_map/ppermute | solution.py:595
  20.0 14.9 %copy-start.3 = (bf16[640,1024]{1,0:T(8,128)(2,1)}, bf16[640,1024]{1,0:T(8,128)(2,1)S(1)}, u32[]{:S(2)}) copy-start(bf16[640,1024]{1,0:T(8,128)(2,1)S(1)} %unit.10.refs_0_.refs_2_) | copy-start | bytes 3932164
  62.4 1.9 copy-start
  64.3 1.6 copy-start.1
  65.9 1.0 copy-start.4
  67.0 1.1 copy-start.6
  68.0 1.9 copy-start.2
  68.1 46.1 %collective-permute-start.2 = (bf16[640,1024]{1,0:T(8,128)(2,1)}, bf16[640,1024]{1,0:T(8,128)(2,1)}, u32[]{:S(2)}, u32[]{:S(2)}) collective-permute-start(bf16[640,1024]{1,0:T(8,128)(2,1)} %copy-done.3), channel_id=1, source_target_pairs={{0,3},{1,4},{2,5},{3,6},{4,7},{5,0},{6,1},{7,2},{8,11},{9,12},{10,... | collective-permute-start | bytes 3932168 | tf_op jit(solution)/shard_map/ppermute | solution.py:595
  71.2 42.9 %all-to-all-start = ((s32[8,8,128]{2,1,0:T(8,128)}), s32[8,8,128]{2,1,0:T(8,128)S(1)}, u32[]{:S(2)}, u32[]{:S(2)}) async-start(s32[8,8,128]{2,1,0:T(8,128)} %sent.1), calls=%async_computation.1 | async-start | bytes 65536 | tf_op jit(solution)/shard_map/all_to_all | solution.py:602
  74.6 154.9 %reduce-scatter.5.cloned.1.call-start = ((), (), s32[]{:S(2)}) async-start(), calls=%async_computation.5 | async-start | bytes 884736 | tf_op jit(solution)/shard_map/reduce_scatter | solution.py:606
  114.1 34.3 %collective-permute-start.3 = (bf16[640,1024]{1,0:T(8,128)(2,1)}, bf16[640,1024]{1,0:T(8,128)(2,1)S(1)}, u32[]{:S(2)}, u32[]{:S(2)}) collective-permute-start(bf16[640,1024]{1,0:T(8,128)(2,1)} %hold.8), channel_id=1, source_target_pairs={{0,7},{1,0},{2,1},{3,2},{4,3},{5,4},{6,5},{7,6},{8,15},{9,8},{10,9... | collective-permute-start | bytes 3932168 | tf_op jit(solution)/shard_map/ppermute | solution.py:595
  114.8 1.1 copy-start.10
  116.0 0.9 copy-start.11
  116.9 65.0 %collective-permute-start.6 = (bf16[640,1024]{1,0:T(8,128)(2,1)}, bf16[640,1024]{1,0:T(8,128)(2,1)S(1)}, u32[]{:S(2)}, u32[]{:S(2)}) collective-permute-start(bf16[640,1024]{1,0:T(8,128)(2,1)} %hold.11), channel_id=1, source_target_pairs={{0,6},{1,7},{2,0},{3,1},{4,2},{5,3},{6,4},{7,5},{8,14},{9,15},{10,... | collective-permute-start | bytes 3932168 | tf_op jit(solution)/shard_map/ppermute | solution.py:595
  117.3 124.2 %collective-permute-start.5 = (bf16[640,1024]{1,0:T(8,128)(2,1)}, bf16[640,1024]{1,0:T(8,128)(2,1)}, u32[]{:S(2)}, u32[]{:S(2)}) collective-permute-start(bf16[640,1024]{1,0:T(8,128)(2,1)} %hold.10), channel_id=1, source_target_pairs={{0,5},{1,6},{2,7},{3,0},{4,1},{5,2},{6,3},{7,4},{8,13},{9,14},{10,... | collective-permute-start | bytes 3932168 | tf_op jit(solution)/shard_map/ppermute | solution.py:595
  148.4 1.1 copy-start.8
  149.5 115.7 %collective-permute-start.4 = (bf16[640,1024]{1,0:T(8,128)(2,1)}, bf16[640,1024]{1,0:T(8,128)(2,1)}, u32[]{:S(2)}, u32[]{:S(2)}) collective-permute-start(bf16[640,1024]{1,0:T(8,128)(2,1)} %hold.9), channel_id=1, source_target_pairs={{0,4},{1,5},{2,6},{3,7},{4,0},{5,1},{6,2},{7,3},{8,12},{9,13},{10,... | collective-permute-start | bytes 3932168 | tf_op jit(solution)/shard_map/ppermute | solution.py:595
  153.0 2.5 copy-start.7
  155.5 5.2 %copy-start.5 = (bf16[640,1024]{1,0:T(8,128)(2,1)S(1)}, bf16[640,1024]{1,0:T(8,128)(2,1)}, u32[]{:S(2)}) copy-start(bf16[640,1024]{1,0:T(8,128)(2,1)} %copy-done.4) | copy-start | bytes 3932164
  166.7 7.4 %copy-start.9 = (bf16[640,1024]{1,0:T(8,128)(2,1)S(1)}, bf16[640,1024]{1,0:T(8,128)(2,1)}, u32[]{:S(2)}) copy-start(bf16[640,1024]{1,0:T(8,128)(2,1)} %copy-done.8) | copy-start | bytes 3932164
  229.4 0.9 copy-start.12
  (1 other events, 0.7 us)
Sparse Core Ops, SparseCore 0:
  68.2 43.3 reduce-scatter.2
  117.0 112.3 reduce-scatter.4
where the time goes:
time: 297 us
  waiting for transfers between devices  134 us (45%)
  Pallas kernels  107 us (36%)
  blocking collectives  20.4 us (7%)
  between operations  14.3 us (5%)
  local copies, waits for them, and re-layouts  12.9 us (4%)
  starting transfers between devices  8.5 us (3%)
    ppermute x7, waiting for transfers between devices, travel(): lax.ppermute(piece, 'docs', [(i, (i + turn) % owner_count) for i in range...  95.5 us
    pallas_call x8, Pallas kernels, gram_step(): pl.pallas_call(functools.partial(gram_kernel, begin, length, wide, len(af...  62 us
    reduce_scatter x1, waiting for transfers between devices, per_device(): lax.psum_scatter(group_share, 'docs', scatter_dimension=0, tiled=True)[0]  38 us
    pallas_call x8, Pallas kernels, unit_piece(): pl.pallas_call(functools.partial(unit_kernel, steps, offset, turn), out_s...  24.1 us
    pallas_call x1, Pallas kernels, slot_sums(): pl.pallas_call(sum_kernel, out_shape=jax.ShapeDtypeStruct((owner_count, p...  14.9 us
    unnamed x30, local copies, waits for them, and re-layouts  12.9 us
    all_gather x1, blocking collectives, per_device(): lax.all_gather(packed, 'grp')  10.3 us
    all_to_all x1, blocking collectives, per_device(): lax.all_to_all(results, 'docs', split_axis=0, concat_axis=0, tiled=True)  10.1 us
  transfers between devices with their start and end apart: 10, of which 5 were waited for; matrix products, arithmetic and copies ran while one was open for 0% of the time, Pallas kernels for 29%

commit v1 on v0

--- a/solution.py
+++ b/solution.py
@@ -105,7 +105,7 @@
     )(starts, me, embeddings, *after)
 
 
-def hold_until(values, arrived):
+def hold_until(values, arrived, mib=8):
     def nothing(*refs):
         pass
 
@@ -115,7 +115,7 @@
         in_specs=[anywhere] * (1 + len(arrived)),
         out_specs=anywhere,
         input_output_aliases={0: 0},
-        compiler_params=params(48),
+        compiler_params=params(mib),
         cost_estimate=brief,
         name="hold",
     )(values, *arrived)
@@ -597,8 +597,9 @@
     chunks = [sent[0]] + [travel(place, sent[place]) for place in (1, 2, 3)]
     sum_labels = summed_labels(starts, slots, owner_count, per_owner, capacity)
     partial_sums = slot_sums(starts, sum_labels, embeddings, per_owner, capacity, sent[1:8])
-    partial_sums = hold_until(partial_sums, chunks[1:3])
-    wire_labels = sent_labels(starts, slots, owner_count, per_owner, capacity, partial_sums)
+    partial_sums = hold_until(partial_sums, chunks[1:3], 62)
+    wire_labels = sent_labels(starts, slots, owner_count, per_owner, capacity, sent[7])
+    wire_labels = hold_until(wire_labels, chunks[1:3])
     got_labels = lax.all_to_all(wire_labels, "docs", split_axis=0, concat_axis=0, tiled=True)
     rows, columns, group_tally = arrived_labels(me, got_labels, turns_of, blocks, width)
     group_share = lax.psum_scatter(partial_sums, "grp", scatter_dimension=1, tiled=True)

time: 297 us -> 291 us (0.980)
  local copies, waits for them, and re-layouts: 12.9 us -> 4.33 us
  waiting for transfers between devices: 134 us -> 137 us
    unnamed x30 -> x16, local copies, waits for them, and re-layouts: 12.9 us -> 4.33 us
  transfers between devices with their start and end apart: 10 -> 10, of which waited for: 5 -> 6; matrix products, arithmetic and copies ran while one was open for 0% -> 0% of each run, Pallas kernels for 29% -> 30%
where the time goes in v1:
time: 291 us
  waiting for transfers between devices  137 us (47%)
  Pallas kernels  106 us (36%)
  blocking collectives  20.2 us (7%)
  between operations  14.3 us (5%)
  starting transfers between devices  9.12 us (3%)
  local copies, waits for them, and re-layouts  4.33 us (1%)
    ppermute x7, waiting for transfers between devices, travel(): lax.ppermute(piece, 'docs', [(i, (i + turn) % owner_count) for i in range...  97.2 us
    pallas_call x8, Pallas kernels, gram_step(): pl.pallas_call(functools.partial(gram_kernel, begin, length, wide, len(af...  62.3 us
    reduce_scatter x1, waiting for transfers between devices, per_device(): lax.psum_scatter(group_share, 'docs', scatter_dimension=0, tiled=True)[0]  39.2 us
    pallas_call x8, Pallas kernels, unit_piece(): pl.pallas_call(functools.partial(unit_kernel, steps, offset, turn), out_s...  23.1 us
    pallas_call x1, Pallas kernels, slot_sums(): pl.pallas_call(sum_kernel, out_shape=jax.ShapeDtypeStruct((owner_count, p...  14.9 us
    all_gather x1, blocking collectives, per_device(): lax.all_gather(packed, 'grp')  10.2 us
    all_to_all x1, blocking collectives, per_device(): lax.all_to_all(results, 'docs', split_axis=0, concat_axis=0, tiled=True)  9.94 us
  transfers between devices with their start and end apart: 10, of which 6 were waited for; matrix products, arithmetic and copies ran while one was open for 0% of the time, Pallas kernels for 30%

profile of v1, /device:TPU:0, one launch (start us, length us, event | category | flops | bytes accessed | tf_op | source)
XLA Modules:
  0.0 290.6 jit_solution(9262100881780327978)
XLA Ops:
  9.5 2.5 unit.8.refs_0_
  12.0 2.5 unit.9.refs_0_.refs_1_
  14.5 3.1 %collective-permute-start.1 = (bf16[640,1024]{1,0:T(8,128)(2,1)S(1)}, bf16[640,1024]{1,0:T(8,128)(2,1)}, u32[]{:S(2)}, u32[]{:S(2)}) collective-permute-start(bf16[640,1024]{1,0:T(8,128)(2,1)S(1)} %unit.9.refs_0_.refs_1_), channel_id=1, source_target_pairs={{0,2},{1,3},{2,4},{3,5},{4,6},{5,7},{6,0},{7,1},{8,10},{9,11},{10,... | collective-permute-start | bytes 3932168 | tf_op jit(solution)/shard_map/ppermute | solution.py:595
  20.0 2.5 unit.11.refs_0_.refs_3_
  22.5 3.6 %unit.12.refs_0_.refs_4_ = bf16[640,1024]{1,0:T(8,128)(2,1)} custom-call(s32[8]{0:T(128)S(1)} %get-tuple-element.26.start_ref, s32[1]{0:T(128)} %bitcast.2.me_ref.refs_6_, f32[4096,1024]{1,0:T(8,128)} %rows_ref.17, bf16[640,1024]{1,0:T(8,128)(2,1)S(1)} %unit.11.refs_0_.refs_3_), custom_call_target="tpu_custom_call" | custom-call | flops 1000 | bytes 1000 | tf_op jit(solution)/shard_map/unit/pallas_call | solution.py:93
  26.1 3.6 %unit.13.refs_0_.refs_5_ = bf16[640,1024]{1,0:T(8,128)(2,1)} custom-call(s32[8]{0:T(128)S(1)} %get-tuple-element.26.start_ref, s32[1]{0:T(128)} %bitcast.2.me_ref.refs_6_, f32[4096,1024]{1,0:T(8,128)} %rows_ref.17, bf16[640,1024]{1,0:T(8,128)(2,1)} %unit.12.refs_0_.refs_4_), custom_call_target="tpu_custom_call" | custom-call | flops 1000 | bytes 1000 | tf_op jit(solution)/shard_map/unit/pallas_call | solution.py:93
  29.7 3.6 %unit.14.refs_6_.after_ref.refs_0_ = bf16[640,1024]{1,0:T(8,128)(2,1)} custom-call(s32[8]{0:T(128)S(1)} %get-tuple-element.26.start_ref, s32[1]{0:T(128)} %bitcast.2.me_ref.refs_6_, f32[4096,1024]{1,0:T(8,128)} %rows_ref.17, bf16[640,1024]{1,0:T(8,128)(2,1)} %unit.13.refs_0_.refs_5_), custom_call_target="tpu_custom_call" | custom-call | flops 1000 | bytes 1000 | tf_op jit(solution)/shard_map/unit/pallas_call | solution.py:93
  33.9 14.9 %sums.1.refs_0_ = f32[8,96,1024]{2,1,0:T(8,128)} custom-call(s32[8]{0:T(128)S(1)} %get-tuple-element.26.start_ref, s32[8,768]{1,0:T(8,128)S(1)} %summed.1.label_ref, f32[4096,1024]{1,0:T(8,128)} %rows_ref.17, bf16[640,1024]{1,0:T(8,128)(2,1)S(1)} %unit.8.refs_0_, bf16[640,1024]{1,0:T(8,128)(2,1)S(1)} %unit.9.refs_0_.refs_1_, ...), custom_call_target="tpu_custom_call" | custom-call | flops 3019898880 | bytes 16777216 | tf_op jit(solution)/shard_map/sums/pallas_call | solution.py:268
  49.3 13.2 %collective-permute-done.refs_1_.refs_0_ = bf16[640,1024]{1,0:T(8,128)(2,1)} collective-permute-done((bf16[640,1024]{1,0:T(8,128)(2,1)S(1)}, bf16[640,1024]{1,0:T(8,128)(2,1)}, u32[]{:S(2)}, u32[]{:S(2)}) %collective-permute-start) | collective-permute-done | bytes 1310752 | tf_op jit(solution)/shard_map/ppermute | solution.py:595
  63.9 3.9 %all-to-all-start = ((s32[8,8,128]{2,1,0:T(8,128)}), s32[8,8,128]{2,1,0:T(8,128)S(1)}, u32[]{:S(2)}, u32[]{:S(2)}) async-start(s32[8,8,128]{2,1,0:T(8,128)} %hold.8), calls=%async_computation.1 | async-start | bytes 65536 | tf_op jit(solution)/shard_map/all_to_all | solution.py:603
  67.8 40.7 %collective-permute-done.2.refs_1_.refs_0_ = bf16[640,1024]{1,0:T(8,128)(2,1)S(1)} collective-permute-done((bf16[640,1024]{1,0:T(8,128)(2,1)}, bf16[640,1024]{1,0:T(8,128)(2,1)S(1)}, u32[]{:S(2)}, u32[]{:S(2)}) %collective-permute-start.2) | collective-permute-done | bytes 1310752 | tf_op jit(solution)/shard_map/ppermute | solution.py:595
  112.6 29.6 %collective-permute-done.3.refs_0_.refs_1_ = bf16[640,1024]{1,0:T(8,128)(2,1)} collective-permute-done((bf16[640,1024]{1,0:T(8,128)(2,1)S(1)}, bf16[640,1024]{1,0:T(8,128)(2,1)}, u32[]{:S(2)}, u32[]{:S(2)}) %collective-permute-start.3) | collective-permute-done | bytes 1310752 | tf_op jit(solution)/shard_map/ppermute | solution.py:595
  145.6 2.5 gram.8
  148.1 5.3 %gram.9 = (f32[40,128]{1,0:T(8,128)S(1)}, bf16[1024,5120]{1,0:T(8,128)(2,1)}) custom-call(bf16[640,1024]{1,0:T(8,128)(2,1)} %collective-permute-done.refs_1_.refs_0_, s32[40,128]{1,0:T(8,128)S(1)} %get-tuple-element.29.refs_1_, s32[5120,128]{1,0:T(8,128)S(1)} %get-tuple-element.30.refs_2_, ...), custom_call_target="tpu_custom_call", output_to_operand_aliasing={{1}: (4, {})} | custom-call | flops 1000 | bytes 1000 | tf_op jit(solution)/shard_map/gram/pallas_call | solution.py:458
  153.5 6.4 %gram.10 = (f32[40,128]{1,0:T(8,128)S(1)}, bf16[1024,5120]{1,0:T(8,128)(2,1)}) custom-call(bf16[640,1024]{1,0:T(8,128)(2,1)} %collective-permute-done.1.refs_2_.refs_0_, s32[40,128]{1,0:T(8,128)S(1)} %get-tuple-element.29.refs_1_, s32[5120,128]{1,0:T(8,128)S(1)} %get-tuple-element.30.refs_2_, ...), custom_call_target="tpu_custom_call", output_to_operand_aliasing={{1}: (4, {})} | custom-call | flops 1000 | bytes 1000 | tf_op jit(solution)/shard_map/gram/pallas_call | solution.py:458
  159.9 7.0 %gram.11 = (f32[40,128]{1,0:T(8,128)S(1)}, bf16[1024,5120]{1,0:T(8,128)(2,1)}) custom-call(bf16[640,1024]{1,0:T(8,128)(2,1)S(1)} %copy-done.1, s32[40,128]{1,0:T(8,128)S(1)} %get-tuple-element.29.refs_1_, s32[5120,128]{1,0:T(8,128)S(1)} %get-tuple-element.30.refs_2_, f32[40,128]{1,0:T(8,128)S(1)} %get-tuple-element.35.refs_3_, ...), custom_call_target="tpu_custom_call", output_to_operand_aliasing={{1}: (4, {})} | custom-call | flops 1000 | bytes 1000 | tf_op jit(solution)/shard_map/gram/pallas_call | solution.py:458
  166.9 7.8 %gram.12 = (f32[40,128]{1,0:T(8,128)S(1)}, bf16[1024,5120]{1,0:T(8,128)(2,1)}) custom-call(bf16[640,1024]{1,0:T(8,128)(2,1)} %collective-permute-done.3.refs_0_.refs_1_, s32[40,128]{1,0:T(8,128)S(1)} %get-tuple-element.29.refs_1_, s32[5120,128]{1,0:T(8,128)S(1)} %get-tuple-element.30.refs_2_, ...), custom_call_target="tpu_custom_call", output_to_operand_aliasing={{1}: (4, {})} | custom-call | flops 1000 | bytes 1000 | tf_op jit(solution)/shard_map/gram/pallas_call | solution.py:458
  174.8 9.5 %gram.13 = (f32[40,128]{1,0:T(8,128)S(1)}, bf16[1024,5120]{1,0:T(8,128)(2,1)}) custom-call(bf16[640,1024]{1,0:T(8,128)(2,1)S(1)} %collective-permute-done.6.refs_0_, s32[40,128]{1,0:T(8,128)S(1)} %get-tuple-element.29.refs_1_, s32[5120,128]{1,0:T(8,128)S(1)} %get-tuple-element.30.refs_2_, ...), custom_call_target="tpu_custom_call", output_to_operand_aliasing={{1}: (4, {})} | custom-call | flops 1000 | bytes 1000 | tf_op jit(solution)/shard_map/gram/pallas_call | solution.py:458
  184.3 39.2 %reduce-scatter.5.cloned.1.call-done = f32[1,24,1024]{2,1,0:T(8,128)} async-done(((f32[8,24,1024]{2,1,0:T(8,128)}), f32[1,24,1024]{2,1,0:T(8,128)}) %reduce-scatter.5.cloned.1.call-update) | async-done | bytes 98320 | tf_op jit(solution)/shard_map/reduce_scatter | solution.py:607
  224.5 10.2 %all-gather = f32[128,1024]{1,0:T(8,128)S(1)} all-gather(f32[32,1024]{1,0:T(8,128)S(1)} %pack.1), channel_id=2, replica_groups=mesh['grp'=4,'docs'=8] {'grp'}, dimensions={0}, use_global_device_ids=true | all-gather | bytes 655360 | tf_op jit(solution)/shard_map/all_gather | solution.py:618
  235.6 10.6 %gram.14 = (f32[40,128]{1,0:T(8,128)S(1)}, bf16[1024,5120]{1,0:T(8,128)(2,1)}) custom-call(bf16[640,1024]{1,0:T(8,128)(2,1)} %collective-permute-done.5.refs_0_, s32[40,128]{1,0:T(8,128)S(1)} %get-tuple-element.29.refs_1_, s32[5120,128]{1,0:T(8,128)S(1)} %get-tuple-element.30.refs_2_, ...), custom_call_target="tpu_custom_call", output_to_operand_aliasing={{1}: (4, {})} | custom-call | flops 1000 | bytes 1000 | tf_op jit(solution)/shard_map/gram/pallas_call | solution.py:458
  246.1 13.3 %collective-permute-done.4.refs_0_ = bf16[640,1024]{1,0:T(8,128)(2,1)} collective-permute-done((bf16[640,1024]{1,0:T(8,128)(2,1)}, bf16[640,1024]{1,0:T(8,128)(2,1)}, u32[]{:S(2)}, u32[]{:S(2)}) %collective-permute-start.4) | collective-permute-done | bytes 1310752 | tf_op jit(solution)/shard_map/ppermute | solution.py:595
  259.5 13.1 %gram.15 = f32[8,16,128]{2,1,0:T(8,128)S(1)} custom-call(bf16[640,1024]{1,0:T(8,128)(2,1)} %collective-permute-done.4.refs_0_, s32[40,128]{1,0:T(8,128)S(1)} %get-tuple-element.29.refs_1_, s32[5120,128]{1,0:T(8,128)S(1)} %get-tuple-element.30.refs_2_, f32[40,128]{1,0:T(8,128)S(1)} %get-tuple-element.45.refs_3_, ...), custom_call_target="tpu_custom_call" | custom-call | flops 1000 | bytes 1000 | tf_op jit(solution)/shard_map/gram/pallas_call | solution.py:458
  272.6 9.9 %all_to_all.10.back_ref = f32[8,16,128]{2,1,0:T(8,128)S(1)} all-to-all(f32[8,16,128]{2,1,0:T(8,128)S(1)} %gram.15), channel_id=1, replica_groups=mesh['grp'=4,'docs'=8] {'docs'}, dimensions={0} | all-to-all | bytes 131072 | tf_op jit(solution)/shard_map/all_to_all | solution.py:625
  (48 shorter events, 17.9 us)
Async XLA Ops:
  7.2 101.9 %reduce-scatter.3.cloned.1.call-start = ((), (), s32[]{:S(2)}) async-start(), calls=%async_computation.4 | async-start | bytes 3932160 | tf_op jit(solution)/shard_map/reduce_scatter | solution.py:605
  7.2 0.7 copy-start.6
  7.9 0.7 copy-start.7
  14.5 34.8 %collective-permute-start.1 = (bf16[640,1024]{1,0:T(8,128)(2,1)S(1)}, bf16[640,1024]{1,0:T(8,128)(2,1)}, u32[]{:S(2)}, u32[]{:S(2)}) collective-permute-start(bf16[640,1024]{1,0:T(8,128)(2,1)S(1)} %unit.9.refs_0_.refs_1_), channel_id=1, source_target_pairs={{0,2},{1,3},{2,4},{3,5},{4,6},{5,7},{6,0},{7,1},{8,10},{9,11},{10,... | collective-permute-start | bytes 3932168 | tf_op jit(solution)/shard_map/ppermute | solution.py:595
  17.5 45.0 %collective-permute-start = (bf16[640,1024]{1,0:T(8,128)(2,1)S(1)}, bf16[640,1024]{1,0:T(8,128)(2,1)}, u32[]{:S(2)}, u32[]{:S(2)}) collective-permute-start(bf16[640,1024]{1,0:T(8,128)(2,1)S(1)} %unit.8.refs_0_), channel_id=1, source_target_pairs={{0,1},{1,2},{2,3},{3,4},{4,5},{5,6},{6,7},{7,0},{8,9},{9,10},{10,1... | collective-permute-start | bytes 3932168 | tf_op jit(solution)/shard_map/ppermute | solution.py:595
  20.0 13.9 %copy-start.2 = (bf16[640,1024]{1,0:T(8,128)(2,1)}, bf16[640,1024]{1,0:T(8,128)(2,1)S(1)}, u32[]{:S(2)}) copy-start(bf16[640,1024]{1,0:T(8,128)(2,1)S(1)} %unit.10.refs_0_.refs_2_) | copy-start | bytes 3932164
  62.5 46.0 %collective-permute-start.2 = (bf16[640,1024]{1,0:T(8,128)(2,1)}, bf16[640,1024]{1,0:T(8,128)(2,1)S(1)}, u32[]{:S(2)}, u32[]{:S(2)}) collective-permute-start(bf16[640,1024]{1,0:T(8,128)(2,1)} %copy-done.2), channel_id=1, source_target_pairs={{0,3},{1,4},{2,5},{3,6},{4,7},{5,0},{6,1},{7,2},{8,11},{9,12},{10,... | collective-permute-start | bytes 3932168 | tf_op jit(solution)/shard_map/ppermute | solution.py:595
  63.9 44.7 %all-to-all-start = ((s32[8,8,128]{2,1,0:T(8,128)}), s32[8,8,128]{2,1,0:T(8,128)S(1)}, u32[]{:S(2)}, u32[]{:S(2)}) async-start(s32[8,8,128]{2,1,0:T(8,128)} %hold.8), calls=%async_computation.1 | async-start | bytes 65536 | tf_op jit(solution)/shard_map/all_to_all | solution.py:603
  67.8 155.8 %reduce-scatter.5.cloned.1.call-start = ((), (), s32[]{:S(2)}) async-start(), calls=%async_computation.5 | async-start | bytes 884736 | tf_op jit(solution)/shard_map/reduce_scatter | solution.py:607
  108.5 3.5 %copy-start = (bf16[640,1024]{1,0:T(8,128)(2,1)}, bf16[640,1024]{1,0:T(8,128)(2,1)S(1)}, u32[]{:S(2)}) copy-start(bf16[640,1024]{1,0:T(8,128)(2,1)S(1)} %collective-permute-done.2.refs_1_.refs_0_) | copy-start | bytes 3932164
  108.5 33.6 %collective-permute-start.3 = (bf16[640,1024]{1,0:T(8,128)(2,1)S(1)}, bf16[640,1024]{1,0:T(8,128)(2,1)}, u32[]{:S(2)}, u32[]{:S(2)}) collective-permute-start(bf16[640,1024]{1,0:T(8,128)(2,1)S(1)} %hold.10), channel_id=1, source_target_pairs={{0,7},{1,0},{2,1},{3,2},{4,3},{5,4},{6,5},{7,6},{8,15},{9,8},{10,9... | collective-permute-start | bytes 3932168 | tf_op jit(solution)/shard_map/ppermute | solution.py:595
  109.1 1.1 copy-start.3
  110.2 0.9 copy-start.4
  111.2 63.6 %collective-permute-start.6 = (bf16[640,1024]{1,0:T(8,128)(2,1)}, bf16[640,1024]{1,0:T(8,128)(2,1)S(1)}, u32[]{:S(2)}, u32[]{:S(2)}) collective-permute-start(bf16[640,1024]{1,0:T(8,128)(2,1)} %hold.13), channel_id=1, source_target_pairs={{0,6},{1,7},{2,0},{3,1},{4,2},{5,3},{6,4},{7,5},{8,14},{9,15},{10,... | collective-permute-start | bytes 3932168 | tf_op jit(solution)/shard_map/ppermute | solution.py:595
  112.0 123.6 %collective-permute-start.5 = (bf16[640,1024]{1,0:T(8,128)(2,1)}, bf16[640,1024]{1,0:T(8,128)(2,1)}, u32[]{:S(2)}, u32[]{:S(2)}) collective-permute-start(bf16[640,1024]{1,0:T(8,128)(2,1)} %hold.12), channel_id=1, source_target_pairs={{0,5},{1,6},{2,7},{3,0},{4,1},{5,2},{6,3},{7,4},{8,13},{9,14},{10,... | collective-permute-start | bytes 3932168 | tf_op jit(solution)/shard_map/ppermute | solution.py:595
  142.2 117.3 %collective-permute-start.4 = (bf16[640,1024]{1,0:T(8,128)(2,1)}, bf16[640,1024]{1,0:T(8,128)(2,1)}, u32[]{:S(2)}, u32[]{:S(2)}) collective-permute-start(bf16[640,1024]{1,0:T(8,128)(2,1)} %hold.11), channel_id=1, source_target_pairs={{0,4},{1,5},{2,6},{3,7},{4,0},{5,1},{6,2},{7,3},{8,12},{9,13},{10,... | collective-permute-start | bytes 3932168 | tf_op jit(solution)/shard_map/ppermute | solution.py:595
  153.4 6.4 %copy-start.1 = (bf16[640,1024]{1,0:T(8,128)(2,1)S(1)}, bf16[640,1024]{1,0:T(8,128)(2,1)}, u32[]{:S(2)}) copy-start(bf16[640,1024]{1,0:T(8,128)(2,1)} %copy-done) | copy-start | bytes 3932164
  223.6 0.9 copy-start.5
Sparse Core Ops, SparseCore 0:
  62.6 43.3 reduce-scatter.2
  111.3 112.2 reduce-scatter.4

commit v2 on v1

--- a/solution.py
+++ b/solution.py
@@ -586,9 +586,13 @@
         assign.reshape(-1, LANES), cluster_slot.reshape(-1, LANES), owner_count, per_owner, row_count - capacity
     )
 
+    last = owner_count - 1
+    cuts = [0, 2 * LANES, capacity] if capacity == padded and blocks > 4 else [0, capacity]
+    parts = [(low, high - low) for low, high in zip(cuts, cuts[1:])]
     sent = []
     for place, turn in enumerate(turns_of):
-        sent.append(unit_piece(starts, me, embeddings, turn, 0, capacity, sent[-1:] if place > 1 else []))
+        for low, length in parts if place == last else [(0, capacity)]:
+            sent.append(unit_piece(starts, me, embeddings, turn, low, length, sent[-1:] if place > 1 else []))
 
     def travel(place, piece):
         turn = turns_of[place]
@@ -596,7 +600,7 @@
 
     chunks = [sent[0]] + [travel(place, sent[place]) for place in (1, 2, 3)]
     sum_labels = summed_labels(starts, slots, owner_count, per_owner, capacity)
-    partial_sums = slot_sums(starts, sum_labels, embeddings, per_owner, capacity, sent[1:8])
+    partial_sums = slot_sums(starts, sum_labels, embeddings, per_owner, capacity, sent[1:9])
     partial_sums = hold_until(partial_sums, chunks[1:3], 62)
     wire_labels = sent_labels(starts, slots, owner_count, per_owner, capacity, sent[7])
     wire_labels = hold_until(wire_labels, chunks[1:3])
@@ -605,22 +609,26 @@
     group_share = lax.psum_scatter(partial_sums, "grp", scatter_dimension=1, tiled=True)
     group_share = hold_until(group_share, [chunks[3], got_labels])
     share = lax.psum_scatter(group_share, "docs", scatter_dimension=0, tiled=True)[0]
-    for place in range(4, owner_count):
-        after = [chunks[4]] if place == owner_count - 1 else [chunks[3], got_labels]
-        chunks.append(travel(place, hold_until(sent[place], after)))
+    for place in range(4, last):
+        chunks.append(travel(place, hold_until(sent[place], [chunks[3], got_labels])))
 
     bests = [jnp.full((owner_count * blocks, LANES), -2.0, jnp.float32)]
     flat = None
-    for place in range(owner_count - 1):
+    for place in range(last):
         after = []
-        if place == owner_count - 2:
+        if place == 4:
+            ends = [travel(last, hold_until(piece, [chunks[last - 2], bests[-1]])) for piece in sent[last:]]
+        if place == last - 1:
             packed = pack_share(share, group_tally, bests[-2:-1])
             centroids, centroid_unit = make_centroids(lax.all_gather(packed, "grp"), per_owner)
             after = [centroid_unit]
         best, flat = gram_step(rows, columns, bests[-1], flat, chunks[place], place * padded, after)
         bests.append(best)
+    for (low, _), chunk in zip(parts[:-1], ends):
+        best, flat = gram_step(rows, columns, bests[-1], flat, chunk, last * padded + low)
+        bests.append(best)
     results = gram_step(
-        rows, columns, bests[-1], flat, chunks[-1], (owner_count - 1) * padded, final=(centroid_unit, me, turns_of)
+        rows, columns, bests[-1], flat, ends[-1], last * padded + cuts[-2], final=(centroid_unit, me, turns_of)
     )
     back = lax.all_to_all(results, "docs", split_axis=0, concat_axis=0, tiled=True)
     near, cosine = place_rows(starts, slots, back, per_owner)

time: 291 us -> 296 us (1.017)
  Pallas kernels: 106 us -> 113 us
  waiting for transfers between devices: 137 us -> 132 us
  starting transfers between devices: 9.12 us -> 12.2 us
    reduce_scatter x1, waiting for transfers between devices: 39.2 us -> 32.1 us  [per_device(): lax.psum_scatter(group_share, 'docs', scatter_dimension=0, tiled=True)[0]]
    pallas_call x8 -> x9, Pallas kernels: 62.3 us -> 66.4 us  [gram_step(): pl.pallas_call(functools.partial(gram_kernel, begin, length, wide, len(af...]
    ppermute x7 -> x8, starting transfers between devices: 5.14 us -> 8.24 us  [travel(): lax.ppermute(piece, 'docs', [(i, (i + turn) % owner_count) for i in range...]
    ppermute x7 -> x8, waiting for transfers between devices: 97.2 us -> 99.9 us  [travel(): lax.ppermute(piece, 'docs', [(i, (i + turn) % owner_count) for i in range...]
    pallas_call x8 -> x9, Pallas kernels: 23.1 us -> 25.6 us  [unit_piece(): pl.pallas_call(functools.partial(unit_kernel, steps, offset, turn), out_s...]
  transfers between devices with their start and end apart: 10 -> 11, of which waited for: 6 -> 6; matrix products, arithmetic and copies ran while one was open for 0% -> 0% of each run, Pallas kernels for 30% -> 32%
where the time goes in v2:
time: 296 us; the launch traced here: 295 us
  waiting for transfers between devices  132 us (45%)
  Pallas kernels  113 us (38%)
  blocking collectives  20.2 us (7%)
  between operations  14.3 us (5%)
  starting transfers between devices  12.2 us (4%)
  local copies, waits for them, and re-layouts  3.63 us (1%)
    ppermute x8, waiting for transfers between devices, travel(): lax.ppermute(piece, 'docs', [(i, (i + turn) % owner_count) for i in range...  99.9 us
    pallas_call x9, Pallas kernels, gram_step(): pl.pallas_call(functools.partial(gram_kernel, begin, length, wide, len(af...  66.4 us
    reduce_scatter x1, waiting for transfers between devices, per_device(): lax.psum_scatter(group_share, 'docs', scatter_dimension=0, tiled=True)[0]  32.1 us
    pallas_call x9, Pallas kernels, unit_piece(): pl.pallas_call(functools.partial(unit_kernel, steps, offset, turn), out_s...  25.6 us
    pallas_call x1, Pallas kernels, slot_sums(): pl.pallas_call(sum_kernel, out_shape=jax.ShapeDtypeStruct((owner_count, p...  14.9 us
    all_gather x1, blocking collectives, per_device(): lax.all_gather(packed, 'grp')  10.3 us
    all_to_all x1, blocking collectives, per_device(): lax.all_to_all(results, 'docs', split_axis=0, concat_axis=0, tiled=True)  9.95 us
    ppermute x8, starting transfers between devices, travel(): lax.ppermute(piece, 'docs', [(i, (i + turn) % owner_count) for i in range...  8.24 us
  transfers between devices with their start and end apart: 11, of which 6 were waited for; matrix products, arithmetic and copies ran while one was open for 0% of the time, Pallas kernels for 32%

profile of v2, /device:TPU:0, one launch (start us, length us, event | category | flops | bytes accessed | tf_op | source)
XLA Modules:
  0.0 295.3 jit_solution(12832182036818151404)
XLA Ops:
  14.5 3.1 %collective-permute-start.1 = (bf16[640,1024]{1,0:T(8,128)(2,1)S(1)}, bf16[640,1024]{1,0:T(8,128)(2,1)}, u32[]{:S(2)}, u32[]{:S(2)}) collective-permute-start(bf16[640,1024]{1,0:T(8,128)(2,1)S(1)} %unit.10.refs_0_.refs_1_), channel_id=1, source_target_pairs={{0,2},{1,3},{2,4},{3,5},{4,6},{5,7},{6,0},{7,1},{8,10},{9,11},{10,... | collective-permute-start | bytes 3932168 | tf_op jit(solution)/shard_map/ppermute | solution.py:599
  20.0 3.6 %unit.12.refs_0_.refs_3_ = bf16[640,1024]{1,0:T(8,128)(2,1)} custom-call(s32[8]{0:T(128)S(1)} %get-tuple-element.28.start_ref, s32[1]{0:T(128)} %bitcast.2.me_ref.refs_6_, f32[4096,1024]{1,0:T(8,128)} %rows_ref.19, bf16[640,1024]{1,0:T(8,128)(2,1)S(1)} %unit.11.refs_0_.refs_2_), custom_call_target="tpu_custom_call" | custom-call | flops 1000 | bytes 1000 | tf_op jit(solution)/shard_map/unit/pallas_call | solution.py:93
  23.6 3.5 %unit.13.refs_0_.refs_4_ = bf16[640,1024]{1,0:T(8,128)(2,1)} custom-call(s32[8]{0:T(128)S(1)} %get-tuple-element.28.start_ref, s32[1]{0:T(128)} %bitcast.2.me_ref.refs_6_, f32[4096,1024]{1,0:T(8,128)} %rows_ref.19, bf16[640,1024]{1,0:T(8,128)(2,1)} %unit.12.refs_0_.refs_3_), custom_call_target="tpu_custom_call" | custom-call | flops 1000 | bytes 1000 | tf_op jit(solution)/shard_map/unit/pallas_call | solution.py:93
  27.2 3.5 %unit.14.refs_0_.refs_5_ = bf16[640,1024]{1,0:T(8,128)(2,1)} custom-call(s32[8]{0:T(128)S(1)} %get-tuple-element.28.start_ref, s32[1]{0:T(128)} %bitcast.2.me_ref.refs_6_, f32[4096,1024]{1,0:T(8,128)} %rows_ref.19, bf16[640,1024]{1,0:T(8,128)(2,1)} %unit.13.refs_0_.refs_4_), custom_call_target="tpu_custom_call" | custom-call | flops 1000 | bytes 1000 | tf_op jit(solution)/shard_map/unit/pallas_call | solution.py:93
  32.7 3.0 %unit.16.refs_7_.refs_0_ = bf16[384,1024]{1,0:T(8,128)(2,1)} custom-call(s32[8]{0:T(128)S(1)} %get-tuple-element.28.start_ref, s32[1]{0:T(128)} %bitcast.2.me_ref.refs_6_, f32[4096,1024]{1,0:T(8,128)} %rows_ref.19, bf16[256,1024]{1,0:T(8,128)(2,1)S(1)} %unit.15.refs_0_.refs_6_.after_ref), custom_call_target="tpu_custom_call" | custom-call | flops 1000 | bytes 1000 | tf_op jit(solution)/shard_map/unit/pallas_call | solution.py:93
  36.4 14.9 %sums.1.refs_0_ = f32[8,96,1024]{2,1,0:T(8,128)} custom-call(s32[8]{0:T(128)S(1)} %get-tuple-element.28.start_ref, s32[8,768]{1,0:T(8,128)S(1)} %summed.1.label_ref, f32[4096,1024]{1,0:T(8,128)} %rows_ref.19, bf16[640,1024]{1,0:T(8,128)(2,1)S(1)} %unit.9.refs_0_, bf16[640,1024]{1,0:T(8,128)(2,1)S(1)} %unit.10.refs_0_.refs_1_, ...), custom_call_target="tpu_custom_call" | custom-call | flops 3019898880 | bytes 16777216 | tf_op jit(solution)/shard_map/sums/pallas_call | solution.py:268
  51.3 11.2 %collective-permute-done.refs_1_.refs_0_ = bf16[640,1024]{1,0:T(8,128)(2,1)} collective-permute-done((bf16[640,1024]{1,0:T(8,128)(2,1)S(1)}, bf16[640,1024]{1,0:T(8,128)(2,1)}, u32[]{:S(2)}, u32[]{:S(2)}) %collective-permute-start) | collective-permute-done | bytes 1310752 | tf_op jit(solution)/shard_map/ppermute | solution.py:599
  65.1 3.9 %all-to-all-start = ((s32[8,8,128]{2,1,0:T(8,128)}), s32[8,8,128]{2,1,0:T(8,128)S(1)}, u32[]{:S(2)}, u32[]{:S(2)}) async-start(s32[8,8,128]{2,1,0:T(8,128)} %hold.9), calls=%async_computation.1 | async-start | bytes 65536 | tf_op jit(solution)/shard_map/all_to_all | solution.py:607
  69.1 40.5 %collective-permute-done.2.refs_1_.refs_0_ = bf16[640,1024]{1,0:T(8,128)(2,1)S(1)} collective-permute-done((bf16[640,1024]{1,0:T(8,128)(2,1)S(1)}, bf16[640,1024]{1,0:T(8,128)(2,1)S(1)}, u32[]{:S(2)}, u32[]{:S(2)}) %collective-permute-start.2) | collective-permute-done | bytes 1310752 | tf_op jit(solution)/shard_map/ppermute | solution.py:599
  117.8 5.3 %gram.10 = (f32[40,128]{1,0:T(8,128)S(1)}, bf16[1024,5120]{1,0:T(8,128)(2,1)}) custom-call(bf16[640,1024]{1,0:T(8,128)(2,1)} %collective-permute-done.refs_1_.refs_0_, s32[40,128]{1,0:T(8,128)S(1)} %get-tuple-element.31.refs_1_, s32[5120,128]{1,0:T(8,128)S(1)} %get-tuple-element.32.refs_2_, ...), custom_call_target="tpu_custom_call", output_to_operand_aliasing={{1}: (4, {})} | custom-call | flops 1000 | bytes 1000 | tf_op jit(solution)/shard_map/gram/pallas_call | solution.py:458
  123.1 6.4 %gram.11 = (f32[40,128]{1,0:T(8,128)S(1)}, bf16[1024,5120]{1,0:T(8,128)(2,1)}) custom-call(bf16[640,1024]{1,0:T(8,128)(2,1)} %collective-permute-done.1.refs_2_.refs_0_, s32[40,128]{1,0:T(8,128)S(1)} %get-tuple-element.31.refs_1_, s32[5120,128]{1,0:T(8,128)S(1)} %get-tuple-element.32.refs_2_, ...), custom_call_target="tpu_custom_call", output_to_operand_aliasing={{1}: (4, {})} | custom-call | flops 1000 | bytes 1000 | tf_op jit(solution)/shard_map/gram/pallas_call | solution.py:458
  129.6 7.0 %gram.12 = (f32[40,128]{1,0:T(8,128)S(1)}, bf16[1024,5120]{1,0:T(8,128)(2,1)}) custom-call(bf16[640,1024]{1,0:T(8,128)(2,1)S(1)} %copy-done.1, s32[40,128]{1,0:T(8,128)S(1)} %get-tuple-element.31.refs_1_, s32[5120,128]{1,0:T(8,128)S(1)} %get-tuple-element.32.refs_2_, f32[40,128]{1,0:T(8,128)S(1)} %get-tuple-element.37.refs_3_, ...), custom_call_target="tpu_custom_call", output_to_operand_aliasing={{1}: (4, {})} | custom-call | flops 1000 | bytes 1000 | tf_op jit(solution)/shard_map/gram/pallas_call | solution.py:458
  136.6 10.1 %collective-permute-done.4.refs_1_.refs_0_ = bf16[640,1024]{1,0:T(8,128)(2,1)} collective-permute-done((bf16[640,1024]{1,0:T(8,128)(2,1)}, bf16[640,1024]{1,0:T(8,128)(2,1)}, u32[]{:S(2)}, u32[]{:S(2)}) %collective-permute-start.4) | collective-permute-done | bytes 1310752 | tf_op jit(solution)/shard_map/ppermute | solution.py:599
  146.7 2.9 collective-permute-start.6
  149.6 24.9 %collective-permute-done.3.refs_0_ = bf16[640,1024]{1,0:T(8,128)(2,1)S(1)} collective-permute-done((bf16[640,1024]{1,0:T(8,128)(2,1)}, bf16[640,1024]{1,0:T(8,128)(2,1)S(1)}, u32[]{:S(2)}, u32[]{:S(2)}) %collective-permute-start.3) | collective-permute-done | bytes 1310752 | tf_op jit(solution)/shard_map/ppermute | solution.py:599
  174.5 7.7 %gram.13 = (f32[40,128]{1,0:T(8,128)S(1)}, bf16[1024,5120]{1,0:T(8,128)(2,1)}) custom-call(bf16[640,1024]{1,0:T(8,128)(2,1)S(1)} %collective-permute-done.3.refs_0_, s32[40,128]{1,0:T(8,128)S(1)} %get-tuple-element.31.refs_1_, s32[5120,128]{1,0:T(8,128)S(1)} %get-tuple-element.32.refs_2_, ...), custom_call_target="tpu_custom_call", output_to_operand_aliasing={{1}: (4, {})} | custom-call | flops 1000 | bytes 1000 | tf_op jit(solution)/shard_map/gram/pallas_call | solution.py:458
  182.2 9.8 %gram.14 = (f32[40,128]{1,0:T(8,128)S(1)}, bf16[1024,5120]{1,0:T(8,128)(2,1)}) custom-call(bf16[640,1024]{1,0:T(8,128)(2,1)} %collective-permute-done.4.refs_1_.refs_0_, s32[40,128]{1,0:T(8,128)S(1)} %get-tuple-element.31.refs_1_, s32[5120,128]{1,0:T(8,128)S(1)} %get-tuple-element.32.refs_2_, ...), custom_call_target="tpu_custom_call", output_to_operand_aliasing={{1}: (4, {})} | custom-call | flops 1000 | bytes 1000 | tf_op jit(solution)/shard_map/gram/pallas_call | solution.py:458
  192.1 32.1 %reduce-scatter.5.cloned.1.call-done = f32[1,24,1024]{2,1,0:T(8,128)} async-done(((f32[8,24,1024]{2,1,0:T(8,128)}), f32[1,24,1024]{2,1,0:T(8,128)}) %reduce-scatter.5.cloned.1.call-update) | async-done | bytes 98320 | tf_op jit(solution)/shard_map/reduce_scatter | solution.py:611
  225.1 10.3 %all-gather = f32[128,1024]{1,0:T(8,128)S(1)} all-gather(f32[32,1024]{1,0:T(8,128)S(1)} %pack.1), channel_id=2, replica_groups=mesh['grp'=4,'docs'=8] {'grp'}, dimensions={0}, use_global_device_ids=true | all-gather | bytes 655360 | tf_op jit(solution)/shard_map/all_gather | solution.py:623
  236.2 10.6 %gram.15 = (f32[40,128]{1,0:T(8,128)S(1)}, bf16[1024,5120]{1,0:T(8,128)(2,1)}) custom-call(bf16[640,1024]{1,0:T(8,128)(2,1)} %collective-permute-done.7.refs_0_, s32[40,128]{1,0:T(8,128)S(1)} %get-tuple-element.31.refs_1_, s32[5120,128]{1,0:T(8,128)S(1)} %get-tuple-element.32.refs_2_, ...), custom_call_target="tpu_custom_call", output_to_operand_aliasing={{1}: (4, {})} | custom-call | flops 1000 | bytes 1000 | tf_op jit(solution)/shard_map/gram/pallas_call | solution.py:458
  246.8 13.4 %collective-permute-done.6.refs_0_ = bf16[256,1024]{1,0:T(8,128)(2,1)} collective-permute-done((bf16[256,1024]{1,0:T(8,128)(2,1)S(1)}, bf16[256,1024]{1,0:T(8,128)(2,1)}, u32[]{:S(2)}, u32[]{:S(2)}) %collective-permute-start.6) | collective-permute-done | bytes 524320 | tf_op jit(solution)/shard_map/ppermute | solution.py:599
  260.1 7.1 %gram.16 = (f32[40,128]{1,0:T(8,128)S(1)}, bf16[1024,5120]{1,0:T(8,128)(2,1)}) custom-call(bf16[256,1024]{1,0:T(8,128)(2,1)} %collective-permute-done.6.refs_0_, s32[40,128]{1,0:T(8,128)S(1)} %get-tuple-element.31.refs_1_, s32[5120,128]{1,0:T(8,128)S(1)} %get-tuple-element.32.refs_2_, ...), custom_call_target="tpu_custom_call", output_to_operand_aliasing={{1}: (4, {})} | custom-call | flops 1000 | bytes 1000 | tf_op jit(solution)/shard_map/gram/pallas_call | solution.py:458
  267.3 9.9 %gram.17 = f32[8,16,128]{2,1,0:T(8,128)S(1)} custom-call(bf16[384,1024]{1,0:T(8,128)(2,1)} %collective-permute-done.5.refs_0_, s32[40,128]{1,0:T(8,128)S(1)} %get-tuple-element.31.refs_1_, s32[5120,128]{1,0:T(8,128)S(1)} %get-tuple-element.32.refs_2_, f32[40,128]{1,0:T(8,128)S(1)} %get-tuple-element.49.refs_3_, ...), custom_call_target="tpu_custom_call" | custom-call | flops 1000 | bytes 1000 | tf_op jit(solution)/shard_map/gram/pallas_call | solution.py:458
  277.2 10.0 %all_to_all.10.back_ref = f32[8,16,128]{2,1,0:T(8,128)S(1)} all-to-all(f32[8,16,128]{2,1,0:T(8,128)S(1)} %gram.17), channel_id=1, replica_groups=mesh['grp'=4,'docs'=8] {'docs'}, dimensions={0} | all-to-all | bytes 131072 | tf_op jit(solution)/shard_map/all_to_all | solution.py:633
  (51 shorter events, 26.3 us)
Async XLA Ops:
  7.2 103.3 %reduce-scatter.3.cloned.1.call-start = ((), (), s32[]{:S(2)}) async-start(), calls=%async_computation.4 | async-start | bytes 3932160 | tf_op jit(solution)/shard_map/reduce_scatter | solution.py:609
  7.2 0.7 copy-start.5
  7.9 0.7 copy-start.6
  14.5 36.9 %collective-permute-start.1 = (bf16[640,1024]{1,0:T(8,128)(2,1)S(1)}, bf16[640,1024]{1,0:T(8,128)(2,1)}, u32[]{:S(2)}, u32[]{:S(2)}) collective-permute-start(bf16[640,1024]{1,0:T(8,128)(2,1)S(1)} %unit.10.refs_0_.refs_1_), channel_id=1, source_target_pairs={{0,2},{1,3},{2,4},{3,5},{4,6},{5,7},{6,0},{7,1},{8,10},{9,11},{10,... | collective-permute-start | bytes 3932168 | tf_op jit(solution)/shard_map/ppermute | solution.py:599
  17.5 45.0 %collective-permute-start = (bf16[640,1024]{1,0:T(8,128)(2,1)S(1)}, bf16[640,1024]{1,0:T(8,128)(2,1)}, u32[]{:S(2)}, u32[]{:S(2)}) collective-permute-start(bf16[640,1024]{1,0:T(8,128)(2,1)S(1)} %unit.9.refs_0_), channel_id=1, source_target_pairs={{0,1},{1,2},{2,3},{3,4},{4,5},{5,6},{6,7},{7,0},{8,9},{9,10},{10,1... | collective-permute-start | bytes 3932168 | tf_op jit(solution)/shard_map/ppermute | solution.py:599
  20.0 16.4 %copy-start.2 = (bf16[640,1024]{1,0:T(8,128)(2,1)}, bf16[640,1024]{1,0:T(8,128)(2,1)S(1)}, u32[]{:S(2)}) copy-start(bf16[640,1024]{1,0:T(8,128)(2,1)S(1)} %unit.11.refs_0_.refs_2_) | copy-start | bytes 3932164
  62.5 1.3 copy-start.3
  63.8 45.7 %collective-permute-start.2 = (bf16[640,1024]{1,0:T(8,128)(2,1)S(1)}, bf16[640,1024]{1,0:T(8,128)(2,1)S(1)}, u32[]{:S(2)}, u32[]{:S(2)}) collective-permute-start(bf16[640,1024]{1,0:T(8,128)(2,1)S(1)} %copy-done.3), channel_id=1, source_target_pairs={{0,3},{1,4},{2,5},{3,6},{4,7},{5,0},{6,1},{7,2},{8,11},{9,12},{10,... | collective-permute-start | bytes 3932168 | tf_op jit(solution)/shard_map/ppermute | solution.py:599
  65.1 44.5 %all-to-all-start = ((s32[8,8,128]{2,1,0:T(8,128)}), s32[8,8,128]{2,1,0:T(8,128)S(1)}, u32[]{:S(2)}, u32[]{:S(2)}) async-start(s32[8,8,128]{2,1,0:T(8,128)} %hold.9), calls=%async_computation.1 | async-start | bytes 65536 | tf_op jit(solution)/shard_map/all_to_all | solution.py:607
  69.0 155.1 %reduce-scatter.5.cloned.1.call-start = ((), (), s32[]{:S(2)}) async-start(), calls=%async_computation.5 | async-start | bytes 884736 | tf_op jit(solution)/shard_map/reduce_scatter | solution.py:611
  109.5 1.1 copy-start
  109.6 37.1 %collective-permute-start.4 = (bf16[640,1024]{1,0:T(8,128)(2,1)}, bf16[640,1024]{1,0:T(8,128)(2,1)}, u32[]{:S(2)}, u32[]{:S(2)}) collective-permute-start(bf16[640,1024]{1,0:T(8,128)(2,1)} %hold.12), channel_id=1, source_target_pairs={{0,6},{1,7},{2,0},{3,1},{4,2},{5,3},{6,4},{7,5},{8,14},{9,15},{10,... | collective-permute-start | bytes 3932168 | tf_op jit(solution)/shard_map/ppermute | solution.py:599
  110.5 64.0 %collective-permute-start.3 = (bf16[640,1024]{1,0:T(8,128)(2,1)}, bf16[640,1024]{1,0:T(8,128)(2,1)S(1)}, u32[]{:S(2)}, u32[]{:S(2)}) collective-permute-start(bf16[640,1024]{1,0:T(8,128)(2,1)} %hold.11), channel_id=1, source_target_pairs={{0,7},{1,0},{2,1},{3,2},{4,3},{5,4},{6,5},{7,6},{8,15},{9,8},{10,9... | collective-permute-start | bytes 3932168 | tf_op jit(solution)/shard_map/ppermute | solution.py:599
  110.6 125.6 %collective-permute-start.7 = (bf16[640,1024]{1,0:T(8,128)(2,1)}, bf16[640,1024]{1,0:T(8,128)(2,1)}, u32[]{:S(2)}, u32[]{:S(2)}) collective-permute-start(bf16[640,1024]{1,0:T(8,128)(2,1)} %hold.15), channel_id=1, source_target_pairs={{0,5},{1,6},{2,7},{3,0},{4,1},{5,2},{6,3},{7,4},{8,13},{9,14},{10,... | collective-permute-start | bytes 3932168 | tf_op jit(solution)/shard_map/ppermute | solution.py:599
  123.1 6.4 %copy-start.1 = (bf16[640,1024]{1,0:T(8,128)(2,1)S(1)}, bf16[640,1024]{1,0:T(8,128)(2,1)}, u32[]{:S(2)}) copy-start(bf16[640,1024]{1,0:T(8,128)(2,1)} %copy-done) | copy-start | bytes 3932164
  146.7 120.6 %collective-permute-start.5 = (bf16[384,1024]{1,0:T(8,128)(2,1)}, bf16[384,1024]{1,0:T(8,128)(2,1)}, u32[]{:S(2)}, u32[]{:S(2)}) collective-permute-start(bf16[384,1024]{1,0:T(8,128)(2,1)} %hold.13), channel_id=1, source_target_pairs={{0,4},{1,5},{2,6},{3,7},{4,0},{5,1},{6,2},{7,3},{8,12},{9,13},{10,... | collective-permute-start | bytes 2359304 | tf_op jit(solution)/shard_map/ppermute | solution.py:599
  146.7 113.5 %collective-permute-start.6 = (bf16[256,1024]{1,0:T(8,128)(2,1)S(1)}, bf16[256,1024]{1,0:T(8,128)(2,1)}, u32[]{:S(2)}, u32[]{:S(2)}) collective-permute-start(bf16[256,1024]{1,0:T(8,128)(2,1)S(1)} %hold.14), channel_id=1, source_target_pairs={{0,4},{1,5},{2,6},{3,7},{4,0},{5,1},{6,2},{7,3},{8,12},{9,13},{10,... | collective-permute-start | bytes 1572872 | tf_op jit(solution)/shard_map/ppermute | solution.py:599
  224.1 0.9 copy-start.4
Sparse Core Ops, SparseCore 0:
  62.6 43.3 reduce-scatter.2
  110.6 113.5 reduce-scatter.4

commit v3 on v1

--- a/solution.py
+++ b/solution.py
@@ -230,6 +230,7 @@
     sum_ref, held, sem = refs[-3:]
     owner_count, per_owner, _ = sum_ref.shape
     window = held.shape[1]
+    widest = float(jnp.finfo(jnp.bfloat16).max)
 
     def copy(owner, slot):
         first = aligned_start(start_ref[owner], rows_ref.shape[0], window)
@@ -249,7 +250,7 @@
         cluster = lax.broadcasted_iota(jnp.int32, (per_owner, window), 0)
         member = (labels == cluster).astype(jnp.float32).astype(jnp.bfloat16)
         values = held[slot]
-        high = values.astype(jnp.bfloat16)
+        high = jnp.clip(values, -widest, widest).astype(jnp.bfloat16)
         rest = values - high.astype(jnp.float32)
         middle = rest.astype(jnp.bfloat16)
         low = (rest - middle.astype(jnp.float32)).astype(jnp.bfloat16)

time: 291 us -> 291 us (level)
  no operation moved by 1% of the time
where the time goes in v3:
time: 291 us
  waiting for transfers between devices  136 us (47%)
  Pallas kernels  106 us (36%)
  blocking collectives  20.2 us (7%)
  between operations  14.3 us (5%)
  starting transfers between devices  9.12 us (3%)
  local copies, waits for them, and re-layouts  4.33 us (1%)
    ppermute x7, waiting for transfers between devices, travel(): lax.ppermute(piece, 'docs', [(i, (i + turn) % owner_count) for i in range...  97 us
    pallas_call x8, Pallas kernels, gram_step(): pl.pallas_call(functools.partial(gram_kernel, begin, length, wide, len(af...  62.3 us
    reduce_scatter x1, waiting for transfers between devices, per_device(): lax.psum_scatter(group_share, 'docs', scatter_dimension=0, tiled=True)[0]  39.2 us
    pallas_call x8, Pallas kernels, unit_piece(): pl.pallas_call(functools.partial(unit_kernel, steps, offset, turn), out_s...  23.1 us
    pallas_call x1, Pallas kernels, slot_sums(): pl.pallas_call(sum_kernel, out_shape=jax.ShapeDtypeStruct((owner_count, p...  15.1 us
    all_gather x1, blocking collectives, per_device(): lax.all_gather(packed, 'grp')  10.2 us
    all_to_all x1, blocking collectives, per_device(): lax.all_to_all(results, 'docs', split_axis=0, concat_axis=0, tiled=True)  9.94 us
  transfers between devices with their start and end apart: 10, of which 6 were waited for; matrix products, arithmetic and copies ran while one was open for 0% of the time, Pallas kernels for 30%

profile of v3, /device:TPU:0, one launch (start us, length us, event | category | flops | bytes accessed | tf_op | source)
XLA Modules:
  0.0 290.6 jit_solution(5382559168597169246)
XLA Ops:
  9.5 2.5 unit.8.refs_0_
  12.0 2.5 unit.9.refs_0_.refs_1_
  14.5 3.1 %collective-permute-start.1 = (bf16[640,1024]{1,0:T(8,128)(2,1)S(1)}, bf16[640,1024]{1,0:T(8,128)(2,1)}, u32[]{:S(2)}, u32[]{:S(2)}) collective-permute-start(bf16[640,1024]{1,0:T(8,128)(2,1)S(1)} %unit.9.refs_0_.refs_1_), channel_id=1, source_target_pairs={{0,2},{1,3},{2,4},{3,5},{4,6},{5,7},{6,0},{7,1},{8,10},{9,11},{10,... | collective-permute-start | bytes 3932168 | tf_op jit(solution)/shard_map/ppermute | solution.py:596
  20.0 2.5 unit.11.refs_0_.refs_3_
  22.5 3.6 %unit.12.refs_0_.refs_4_ = bf16[640,1024]{1,0:T(8,128)(2,1)} custom-call(s32[8]{0:T(128)S(1)} %get-tuple-element.26.start_ref, s32[1]{0:T(128)} %bitcast.2.me_ref.refs_6_, f32[4096,1024]{1,0:T(8,128)} %rows_ref.17, bf16[640,1024]{1,0:T(8,128)(2,1)S(1)} %unit.11.refs_0_.refs_3_), custom_call_target="tpu_custom_call" | custom-call | flops 1000 | bytes 1000 | tf_op jit(solution)/shard_map/unit/pallas_call | solution.py:93
  26.1 3.6 %unit.13.refs_0_.refs_5_ = bf16[640,1024]{1,0:T(8,128)(2,1)} custom-call(s32[8]{0:T(128)S(1)} %get-tuple-element.26.start_ref, s32[1]{0:T(128)} %bitcast.2.me_ref.refs_6_, f32[4096,1024]{1,0:T(8,128)} %rows_ref.17, bf16[640,1024]{1,0:T(8,128)(2,1)} %unit.12.refs_0_.refs_4_), custom_call_target="tpu_custom_call" | custom-call | flops 1000 | bytes 1000 | tf_op jit(solution)/shard_map/unit/pallas_call | solution.py:93
  29.7 3.6 %unit.14.refs_6_.after_ref.refs_0_ = bf16[640,1024]{1,0:T(8,128)(2,1)} custom-call(s32[8]{0:T(128)S(1)} %get-tuple-element.26.start_ref, s32[1]{0:T(128)} %bitcast.2.me_ref.refs_6_, f32[4096,1024]{1,0:T(8,128)} %rows_ref.17, bf16[640,1024]{1,0:T(8,128)(2,1)} %unit.13.refs_0_.refs_5_), custom_call_target="tpu_custom_call" | custom-call | flops 1000 | bytes 1000 | tf_op jit(solution)/shard_map/unit/pallas_call | solution.py:93
  33.9 15.1 %sums.1.refs_0_ = f32[8,96,1024]{2,1,0:T(8,128)} custom-call(s32[8]{0:T(128)S(1)} %get-tuple-element.26.start_ref, s32[8,768]{1,0:T(8,128)S(1)} %summed.1.label_ref, f32[4096,1024]{1,0:T(8,128)} %rows_ref.17, bf16[640,1024]{1,0:T(8,128)(2,1)S(1)} %unit.8.refs_0_, bf16[640,1024]{1,0:T(8,128)(2,1)S(1)} %unit.9.refs_0_.refs_1_, ...), custom_call_target="tpu_custom_call" | custom-call | flops 3019898880 | bytes 16777216 | tf_op jit(solution)/shard_map/sums/pallas_call | solution.py:269
  49.3 13.2 %collective-permute-done.refs_1_.refs_0_ = bf16[640,1024]{1,0:T(8,128)(2,1)} collective-permute-done((bf16[640,1024]{1,0:T(8,128)(2,1)S(1)}, bf16[640,1024]{1,0:T(8,128)(2,1)}, u32[]{:S(2)}, u32[]{:S(2)}) %collective-permute-start) | collective-permute-done | bytes 1310752 | tf_op jit(solution)/shard_map/ppermute | solution.py:596
  63.9 3.9 %all-to-all-start = ((s32[8,8,128]{2,1,0:T(8,128)}), s32[8,8,128]{2,1,0:T(8,128)S(1)}, u32[]{:S(2)}, u32[]{:S(2)}) async-start(s32[8,8,128]{2,1,0:T(8,128)} %hold.8), calls=%async_computation.1 | async-start | bytes 65536 | tf_op jit(solution)/shard_map/all_to_all | solution.py:604
  67.8 40.7 %collective-permute-done.2.refs_1_.refs_0_ = bf16[640,1024]{1,0:T(8,128)(2,1)S(1)} collective-permute-done((bf16[640,1024]{1,0:T(8,128)(2,1)}, bf16[640,1024]{1,0:T(8,128)(2,1)S(1)}, u32[]{:S(2)}, u32[]{:S(2)}) %collective-permute-start.2) | collective-permute-done | bytes 1310752 | tf_op jit(solution)/shard_map/ppermute | solution.py:596
  112.6 29.6 %collective-permute-done.3.refs_0_.refs_1_ = bf16[640,1024]{1,0:T(8,128)(2,1)} collective-permute-done((bf16[640,1024]{1,0:T(8,128)(2,1)S(1)}, bf16[640,1024]{1,0:T(8,128)(2,1)}, u32[]{:S(2)}, u32[]{:S(2)}) %collective-permute-start.3) | collective-permute-done | bytes 1310752 | tf_op jit(solution)/shard_map/ppermute | solution.py:596
  145.6 2.5 gram.8
  148.1 5.3 %gram.9 = (f32[40,128]{1,0:T(8,128)S(1)}, bf16[1024,5120]{1,0:T(8,128)(2,1)}) custom-call(bf16[640,1024]{1,0:T(8,128)(2,1)} %collective-permute-done.refs_1_.refs_0_, s32[40,128]{1,0:T(8,128)S(1)} %get-tuple-element.29.refs_1_, s32[5120,128]{1,0:T(8,128)S(1)} %get-tuple-element.30.refs_2_, ...), custom_call_target="tpu_custom_call", output_to_operand_aliasing={{1}: (4, {})} | custom-call | flops 1000 | bytes 1000 | tf_op jit(solution)/shard_map/gram/pallas_call | solution.py:459
  153.5 6.4 %gram.10 = (f32[40,128]{1,0:T(8,128)S(1)}, bf16[1024,5120]{1,0:T(8,128)(2,1)}) custom-call(bf16[640,1024]{1,0:T(8,128)(2,1)} %collective-permute-done.1.refs_2_.refs_0_, s32[40,128]{1,0:T(8,128)S(1)} %get-tuple-element.29.refs_1_, s32[5120,128]{1,0:T(8,128)S(1)} %get-tuple-element.30.refs_2_, ...), custom_call_target="tpu_custom_call", output_to_operand_aliasing={{1}: (4, {})} | custom-call | flops 1000 | bytes 1000 | tf_op jit(solution)/shard_map/gram/pallas_call | solution.py:459
  159.9 7.0 %gram.11 = (f32[40,128]{1,0:T(8,128)S(1)}, bf16[1024,5120]{1,0:T(8,128)(2,1)}) custom-call(bf16[640,1024]{1,0:T(8,128)(2,1)S(1)} %copy-done.1, s32[40,128]{1,0:T(8,128)S(1)} %get-tuple-element.29.refs_1_, s32[5120,128]{1,0:T(8,128)S(1)} %get-tuple-element.30.refs_2_, f32[40,128]{1,0:T(8,128)S(1)} %get-tuple-element.35.refs_3_, ...), custom_call_target="tpu_custom_call", output_to_operand_aliasing={{1}: (4, {})} | custom-call | flops 1000 | bytes 1000 | tf_op jit(solution)/shard_map/gram/pallas_call | solution.py:459
  166.9 7.8 %gram.12 = (f32[40,128]{1,0:T(8,128)S(1)}, bf16[1024,5120]{1,0:T(8,128)(2,1)}) custom-call(bf16[640,1024]{1,0:T(8,128)(2,1)} %collective-permute-done.3.refs_0_.refs_1_, s32[40,128]{1,0:T(8,128)S(1)} %get-tuple-element.29.refs_1_, s32[5120,128]{1,0:T(8,128)S(1)} %get-tuple-element.30.refs_2_, ...), custom_call_target="tpu_custom_call", output_to_operand_aliasing={{1}: (4, {})} | custom-call | flops 1000 | bytes 1000 | tf_op jit(solution)/shard_map/gram/pallas_call | solution.py:459
  174.8 9.5 %gram.13 = (f32[40,128]{1,0:T(8,128)S(1)}, bf16[1024,5120]{1,0:T(8,128)(2,1)}) custom-call(bf16[640,1024]{1,0:T(8,128)(2,1)S(1)} %collective-permute-done.6.refs_0_, s32[40,128]{1,0:T(8,128)S(1)} %get-tuple-element.29.refs_1_, s32[5120,128]{1,0:T(8,128)S(1)} %get-tuple-element.30.refs_2_, ...), custom_call_target="tpu_custom_call", output_to_operand_aliasing={{1}: (4, {})} | custom-call | flops 1000 | bytes 1000 | tf_op jit(solution)/shard_map/gram/pallas_call | solution.py:459
  184.3 39.2 %reduce-scatter.5.cloned.1.call-done = f32[1,24,1024]{2,1,0:T(8,128)} async-done(((f32[8,24,1024]{2,1,0:T(8,128)}), f32[1,24,1024]{2,1,0:T(8,128)}) %reduce-scatter.5.cloned.1.call-update) | async-done | bytes 98320 | tf_op jit(solution)/shard_map/reduce_scatter | solution.py:608
  224.5 10.2 %all-gather = f32[128,1024]{1,0:T(8,128)S(1)} all-gather(f32[32,1024]{1,0:T(8,128)S(1)} %pack.1), channel_id=2, replica_groups=mesh['grp'=4,'docs'=8] {'grp'}, dimensions={0}, use_global_device_ids=true | all-gather | bytes 655360 | tf_op jit(solution)/shard_map/all_gather | solution.py:619
  235.6 10.6 %gram.14 = (f32[40,128]{1,0:T(8,128)S(1)}, bf16[1024,5120]{1,0:T(8,128)(2,1)}) custom-call(bf16[640,1024]{1,0:T(8,128)(2,1)} %collective-permute-done.5.refs_0_, s32[40,128]{1,0:T(8,128)S(1)} %get-tuple-element.29.refs_1_, s32[5120,128]{1,0:T(8,128)S(1)} %get-tuple-element.30.refs_2_, ...), custom_call_target="tpu_custom_call", output_to_operand_aliasing={{1}: (4, {})} | custom-call | flops 1000 | bytes 1000 | tf_op jit(solution)/shard_map/gram/pallas_call | solution.py:459
  246.1 13.3 %collective-permute-done.4.refs_0_ = bf16[640,1024]{1,0:T(8,128)(2,1)} collective-permute-done((bf16[640,1024]{1,0:T(8,128)(2,1)}, bf16[640,1024]{1,0:T(8,128)(2,1)}, u32[]{:S(2)}, u32[]{:S(2)}) %collective-permute-start.4) | collective-permute-done | bytes 1310752 | tf_op jit(solution)/shard_map/ppermute | solution.py:596
  259.5 13.1 %gram.15 = f32[8,16,128]{2,1,0:T(8,128)S(1)} custom-call(bf16[640,1024]{1,0:T(8,128)(2,1)} %collective-permute-done.4.refs_0_, s32[40,128]{1,0:T(8,128)S(1)} %get-tuple-element.29.refs_1_, s32[5120,128]{1,0:T(8,128)S(1)} %get-tuple-element.30.refs_2_, f32[40,128]{1,0:T(8,128)S(1)} %get-tuple-element.45.refs_3_, ...), custom_call_target="tpu_custom_call" | custom-call | flops 1000 | bytes 1000 | tf_op jit(solution)/shard_map/gram/pallas_call | solution.py:459
  272.6 9.9 %all_to_all.10.back_ref = f32[8,16,128]{2,1,0:T(8,128)S(1)} all-to-all(f32[8,16,128]{2,1,0:T(8,128)S(1)} %gram.15), channel_id=1, replica_groups=mesh['grp'=4,'docs'=8] {'docs'}, dimensions={0} | all-to-all | bytes 131072 | tf_op jit(solution)/shard_map/all_to_all | solution.py:626
  (48 shorter events, 17.7 us)
Async XLA Ops:
  7.2 101.9 %reduce-scatter.3.cloned.1.call-start = ((), (), s32[]{:S(2)}) async-start(), calls=%async_computation.4 | async-start | bytes 3932160 | tf_op jit(solution)/shard_map/reduce_scatter | solution.py:606
  7.2 0.7 copy-start.6
  7.9 0.7 copy-start.7
  14.5 34.8 %collective-permute-start.1 = (bf16[640,1024]{1,0:T(8,128)(2,1)S(1)}, bf16[640,1024]{1,0:T(8,128)(2,1)}, u32[]{:S(2)}, u32[]{:S(2)}) collective-permute-start(bf16[640,1024]{1,0:T(8,128)(2,1)S(1)} %unit.9.refs_0_.refs_1_), channel_id=1, source_target_pairs={{0,2},{1,3},{2,4},{3,5},{4,6},{5,7},{6,0},{7,1},{8,10},{9,11},{10,... | collective-permute-start | bytes 3932168 | tf_op jit(solution)/shard_map/ppermute | solution.py:596
  17.5 45.0 %collective-permute-start = (bf16[640,1024]{1,0:T(8,128)(2,1)S(1)}, bf16[640,1024]{1,0:T(8,128)(2,1)}, u32[]{:S(2)}, u32[]{:S(2)}) collective-permute-start(bf16[640,1024]{1,0:T(8,128)(2,1)S(1)} %unit.8.refs_0_), channel_id=1, source_target_pairs={{0,1},{1,2},{2,3},{3,4},{4,5},{5,6},{6,7},{7,0},{8,9},{9,10},{10,1... | collective-permute-start | bytes 3932168 | tf_op jit(solution)/shard_map/ppermute | solution.py:596
  20.0 13.9 %copy-start.2 = (bf16[640,1024]{1,0:T(8,128)(2,1)}, bf16[640,1024]{1,0:T(8,128)(2,1)S(1)}, u32[]{:S(2)}) copy-start(bf16[640,1024]{1,0:T(8,128)(2,1)S(1)} %unit.10.refs_0_.refs_2_) | copy-start | bytes 3932164
  62.5 46.0 %collective-permute-start.2 = (bf16[640,1024]{1,0:T(8,128)(2,1)}, bf16[640,1024]{1,0:T(8,128)(2,1)S(1)}, u32[]{:S(2)}, u32[]{:S(2)}) collective-permute-start(bf16[640,1024]{1,0:T(8,128)(2,1)} %copy-done.2), channel_id=1, source_target_pairs={{0,3},{1,4},{2,5},{3,6},{4,7},{5,0},{6,1},{7,2},{8,11},{9,12},{10,... | collective-permute-start | bytes 3932168 | tf_op jit(solution)/shard_map/ppermute | solution.py:596
  63.9 44.7 %all-to-all-start = ((s32[8,8,128]{2,1,0:T(8,128)}), s32[8,8,128]{2,1,0:T(8,128)S(1)}, u32[]{:S(2)}, u32[]{:S(2)}) async-start(s32[8,8,128]{2,1,0:T(8,128)} %hold.8), calls=%async_computation.1 | async-start | bytes 65536 | tf_op jit(solution)/shard_map/all_to_all | solution.py:604
  67.8 155.8 %reduce-scatter.5.cloned.1.call-start = ((), (), s32[]{:S(2)}) async-start(), calls=%async_computation.5 | async-start | bytes 884736 | tf_op jit(solution)/shard_map/reduce_scatter | solution.py:608
  108.5 3.5 %copy-start = (bf16[640,1024]{1,0:T(8,128)(2,1)}, bf16[640,1024]{1,0:T(8,128)(2,1)S(1)}, u32[]{:S(2)}) copy-start(bf16[640,1024]{1,0:T(8,128)(2,1)S(1)} %collective-permute-done.2.refs_1_.refs_0_) | copy-start | bytes 3932164
  108.5 33.6 %collective-permute-start.3 = (bf16[640,1024]{1,0:T(8,128)(2,1)S(1)}, bf16[640,1024]{1,0:T(8,128)(2,1)}, u32[]{:S(2)}, u32[]{:S(2)}) collective-permute-start(bf16[640,1024]{1,0:T(8,128)(2,1)S(1)} %hold.10), channel_id=1, source_target_pairs={{0,7},{1,0},{2,1},{3,2},{4,3},{5,4},{6,5},{7,6},{8,15},{9,8},{10,9... | collective-permute-start | bytes 3932168 | tf_op jit(solution)/shard_map/ppermute | solution.py:596
  109.1 1.1 copy-start.3
  110.2 0.9 copy-start.4
  111.2 63.6 %collective-permute-start.6 = (bf16[640,1024]{1,0:T(8,128)(2,1)}, bf16[640,1024]{1,0:T(8,128)(2,1)S(1)}, u32[]{:S(2)}, u32[]{:S(2)}) collective-permute-start(bf16[640,1024]{1,0:T(8,128)(2,1)} %hold.13), channel_id=1, source_target_pairs={{0,6},{1,7},{2,0},{3,1},{4,2},{5,3},{6,4},{7,5},{8,14},{9,15},{10,... | collective-permute-start | bytes 3932168 | tf_op jit(solution)/shard_map/ppermute | solution.py:596
  112.0 123.6 %collective-permute-start.5 = (bf16[640,1024]{1,0:T(8,128)(2,1)}, bf16[640,1024]{1,0:T(8,128)(2,1)}, u32[]{:S(2)}, u32[]{:S(2)}) collective-permute-start(bf16[640,1024]{1,0:T(8,128)(2,1)} %hold.12), channel_id=1, source_target_pairs={{0,5},{1,6},{2,7},{3,0},{4,1},{5,2},{6,3},{7,4},{8,13},{9,14},{10,... | collective-permute-start | bytes 3932168 | tf_op jit(solution)/shard_map/ppermute | solution.py:596
  142.2 117.3 %collective-permute-start.4 = (bf16[640,1024]{1,0:T(8,128)(2,1)}, bf16[640,1024]{1,0:T(8,128)(2,1)}, u32[]{:S(2)}, u32[]{:S(2)}) collective-permute-start(bf16[640,1024]{1,0:T(8,128)(2,1)} %hold.11), channel_id=1, source_target_pairs={{0,4},{1,5},{2,6},{3,7},{4,0},{5,1},{6,2},{7,3},{8,12},{9,13},{10,... | collective-permute-start | bytes 3932168 | tf_op jit(solution)/shard_map/ppermute | solution.py:596
  153.4 6.4 %copy-start.1 = (bf16[640,1024]{1,0:T(8,128)(2,1)S(1)}, bf16[640,1024]{1,0:T(8,128)(2,1)}, u32[]{:S(2)}) copy-start(bf16[640,1024]{1,0:T(8,128)(2,1)} %copy-done) | copy-start | bytes 3932164
  223.6 0.9 copy-start.5
Sparse Core Ops, SparseCore 0:
  62.6 43.3 reduce-scatter.2
  111.3 112.2 reduce-scatter.4

commit v4 on v3

--- a/solution.py
+++ b/solution.py
@@ -569,7 +569,7 @@
 def turns(count):
     order = sorted(range(count), key=lambda turn: (min(turn, count - turn), turn))
     if count == 8:
-        order = [0, 1, 2, 3, 7, 6, 5, 4]
+        order = [0, 2, 1, 3, 7, 6, 5, 4]
     return order
 
 

time: 291 us -> 291 us (level)
  waiting for transfers between devices: 136 us -> 121 us
  starting transfers between devices: 9.12 us -> 22.9 us
    ppermute x7, waiting for transfers between devices: 97 us -> 81.7 us  [travel(): lax.ppermute(piece, 'docs', [(i, (i + turn) % owner_count) for i in range...]
    ppermute x7, starting transfers between devices: 5.14 us -> 18 us  [travel(): lax.ppermute(piece, 'docs', [(i, (i + turn) % owner_count) for i in range...]
  transfers between devices with their start and end apart: 10 -> 10, of which waited for: 6 -> 5; matrix products, arithmetic and copies ran while one was open for 0% -> 0% of each run, Pallas kernels for 30% -> 30%
where the time goes in v4:
time: 291 us; the launch traced here: 290 us
  waiting for transfers between devices  121 us (42%)
  Pallas kernels  106 us (36%)
  starting transfers between devices  22.9 us (8%)
  blocking collectives  20.5 us (7%)
  between operations  14.3 us (5%)
  local copies, waits for them, and re-layouts  4.33 us (1%)
    ppermute x7, waiting for transfers between devices, travel(): lax.ppermute(piece, 'docs', [(i, (i + turn) % owner_count) for i in range...  81.7 us
    pallas_call x8, Pallas kernels, gram_step(): pl.pallas_call(functools.partial(gram_kernel, begin, length, wide, len(af...  62.3 us
    reduce_scatter x1, waiting for transfers between devices, per_device(): lax.psum_scatter(group_share, 'docs', scatter_dimension=0, tiled=True)[0]  39.6 us
    pallas_call x8, Pallas kernels, unit_piece(): pl.pallas_call(functools.partial(unit_kernel, steps, offset, turn), out_s...  23.1 us
    ppermute x7, starting transfers between devices, travel(): lax.ppermute(piece, 'docs', [(i, (i + turn) % owner_count) for i in range...  18 us
    pallas_call x1, Pallas kernels, slot_sums(): pl.pallas_call(sum_kernel, out_shape=jax.ShapeDtypeStruct((owner_count, p...  15.1 us
    all_gather x1, blocking collectives, per_device(): lax.all_gather(packed, 'grp')  10.2 us
    all_to_all x1, blocking collectives, per_device(): lax.all_to_all(results, 'docs', split_axis=0, concat_axis=0, tiled=True)  10.2 us
  transfers between devices with their start and end apart: 10, of which 5 were waited for; matrix products, arithmetic and copies ran while one was open for 0% of the time, Pallas kernels for 30%

profile of v4, /device:TPU:0, one launch (start us, length us, event | category | flops | bytes accessed | tf_op | source)
XLA Modules:
  0.0 289.9 jit_solution(12568639943141774505)
XLA Ops:
  9.5 2.5 unit.8.refs_0_
  12.0 2.5 unit.9.refs_0_.refs_1_
  15.0 2.6 collective-permute-start
  20.1 2.5 unit.11.refs_0_.refs_3_
  22.6 3.6 %unit.12.refs_0_.refs_4_ = bf16[640,1024]{1,0:T(8,128)(2,1)} custom-call(s32[8]{0:T(128)S(1)} %get-tuple-element.26.start_ref, s32[1]{0:T(128)} %bitcast.2.me_ref.refs_6_, f32[4096,1024]{1,0:T(8,128)} %rows_ref.17, bf16[640,1024]{1,0:T(8,128)(2,1)S(1)} %unit.11.refs_0_.refs_3_), custom_call_target="tpu_custom_call" | custom-call | flops 1000 | bytes 1000 | tf_op jit(solution)/shard_map/unit/pallas_call | solution.py:93
  26.2 3.6 %unit.13.refs_0_.refs_5_ = bf16[640,1024]{1,0:T(8,128)(2,1)} custom-call(s32[8]{0:T(128)S(1)} %get-tuple-element.26.start_ref, s32[1]{0:T(128)} %bitcast.2.me_ref.refs_6_, f32[4096,1024]{1,0:T(8,128)} %rows_ref.17, bf16[640,1024]{1,0:T(8,128)(2,1)} %unit.12.refs_0_.refs_4_), custom_call_target="tpu_custom_call" | custom-call | flops 1000 | bytes 1000 | tf_op jit(solution)/shard_map/unit/pallas_call | solution.py:93
  29.7 3.6 %unit.14.refs_6_.after_ref.refs_0_ = bf16[640,1024]{1,0:T(8,128)(2,1)} custom-call(s32[8]{0:T(128)S(1)} %get-tuple-element.26.start_ref, s32[1]{0:T(128)} %bitcast.2.me_ref.refs_6_, f32[4096,1024]{1,0:T(8,128)} %rows_ref.17, bf16[640,1024]{1,0:T(8,128)(2,1)} %unit.13.refs_0_.refs_5_), custom_call_target="tpu_custom_call" | custom-call | flops 1000 | bytes 1000 | tf_op jit(solution)/shard_map/unit/pallas_call | solution.py:93
  34.0 15.1 %sums.1.refs_0_ = f32[8,96,1024]{2,1,0:T(8,128)} custom-call(s32[8]{0:T(128)S(1)} %get-tuple-element.26.start_ref, s32[8,768]{1,0:T(8,128)S(1)} %summed.1.label_ref, f32[4096,1024]{1,0:T(8,128)} %rows_ref.17, bf16[640,1024]{1,0:T(8,128)(2,1)S(1)} %unit.8.refs_0_, bf16[640,1024]{1,0:T(8,128)(2,1)S(1)} %unit.9.refs_0_.refs_1_, ...), custom_call_target="tpu_custom_call" | custom-call | flops 3019898880 | bytes 16777216 | tf_op jit(solution)/shard_map/sums/pallas_call | solution.py:269
  49.4 12.9 %collective-permute-start.2 = (bf16[640,1024]{1,0:T(8,128)(2,1)}, bf16[640,1024]{1,0:T(8,128)(2,1)S(1)}, u32[]{:S(2)}, u32[]{:S(2)}) collective-permute-start(bf16[640,1024]{1,0:T(8,128)(2,1)} %copy-done.2), channel_id=1, source_target_pairs={{0,3},{1,4},{2,5},{3,6},{4,7},{5,0},{6,1},{7,2},{8,11},{9,12},{10,... | collective-permute-start | bytes 3932168 | tf_op jit(solution)/shard_map/ppermute | solution.py:596
  63.6 4.8 %all-to-all-start = ((s32[8,8,128]{2,1,0:T(8,128)}), s32[8,8,128]{2,1,0:T(8,128)S(1)}, u32[]{:S(2)}, u32[]{:S(2)}) async-start(s32[8,8,128]{2,1,0:T(8,128)} %hold.8), calls=%async_computation.1 | async-start | bytes 65536 | tf_op jit(solution)/shard_map/all_to_all | solution.py:604
  68.4 39.0 %collective-permute-done.2.refs_1_.refs_0_ = bf16[640,1024]{1,0:T(8,128)(2,1)S(1)} collective-permute-done((bf16[640,1024]{1,0:T(8,128)(2,1)}, bf16[640,1024]{1,0:T(8,128)(2,1)S(1)}, u32[]{:S(2)}, u32[]{:S(2)}) %collective-permute-start.2) | collective-permute-done | bytes 1310752 | tf_op jit(solution)/shard_map/ppermute | solution.py:596
  111.5 29.5 %collective-permute-done.3.refs_0_.refs_1_ = bf16[640,1024]{1,0:T(8,128)(2,1)} collective-permute-done((bf16[640,1024]{1,0:T(8,128)(2,1)S(1)}, bf16[640,1024]{1,0:T(8,128)(2,1)}, u32[]{:S(2)}, u32[]{:S(2)}) %collective-permute-start.3) | collective-permute-done | bytes 1310752 | tf_op jit(solution)/shard_map/ppermute | solution.py:596
  144.5 2.5 gram.8
  147.0 5.3 %gram.9 = (f32[40,128]{1,0:T(8,128)S(1)}, bf16[1024,5120]{1,0:T(8,128)(2,1)}) custom-call(bf16[640,1024]{1,0:T(8,128)(2,1)} %collective-permute-done.refs_1_.refs_0_, s32[40,128]{1,0:T(8,128)S(1)} %get-tuple-element.29.refs_1_, s32[5120,128]{1,0:T(8,128)S(1)} %get-tuple-element.30.refs_2_, ...), custom_call_target="tpu_custom_call", output_to_operand_aliasing={{1}: (4, {})} | custom-call | flops 1000 | bytes 1000 | tf_op jit(solution)/shard_map/gram/pallas_call | solution.py:459
  152.3 6.4 %gram.10 = (f32[40,128]{1,0:T(8,128)S(1)}, bf16[1024,5120]{1,0:T(8,128)(2,1)}) custom-call(bf16[640,1024]{1,0:T(8,128)(2,1)} %collective-permute-done.1.refs_2_.refs_0_, s32[40,128]{1,0:T(8,128)S(1)} %get-tuple-element.29.refs_1_, s32[5120,128]{1,0:T(8,128)S(1)} %get-tuple-element.30.refs_2_, ...), custom_call_target="tpu_custom_call", output_to_operand_aliasing={{1}: (4, {})} | custom-call | flops 1000 | bytes 1000 | tf_op jit(solution)/shard_map/gram/pallas_call | solution.py:459
  158.7 7.0 %gram.11 = (f32[40,128]{1,0:T(8,128)S(1)}, bf16[1024,5120]{1,0:T(8,128)(2,1)}) custom-call(bf16[640,1024]{1,0:T(8,128)(2,1)S(1)} %copy-done.1, s32[40,128]{1,0:T(8,128)S(1)} %get-tuple-element.29.refs_1_, s32[5120,128]{1,0:T(8,128)S(1)} %get-tuple-element.30.refs_2_, f32[40,128]{1,0:T(8,128)S(1)} %get-tuple-element.35.refs_3_, ...), custom_call_target="tpu_custom_call", output_to_operand_aliasing={{1}: (4, {})} | custom-call | flops 1000 | bytes 1000 | tf_op jit(solution)/shard_map/gram/pallas_call | solution.py:459
  165.8 7.8 %gram.12 = (f32[40,128]{1,0:T(8,128)S(1)}, bf16[1024,5120]{1,0:T(8,128)(2,1)}) custom-call(bf16[640,1024]{1,0:T(8,128)(2,1)} %collective-permute-done.3.refs_0_.refs_1_, s32[40,128]{1,0:T(8,128)S(1)} %get-tuple-element.29.refs_1_, s32[5120,128]{1,0:T(8,128)S(1)} %get-tuple-element.30.refs_2_, ...), custom_call_target="tpu_custom_call", output_to_operand_aliasing={{1}: (4, {})} | custom-call | flops 1000 | bytes 1000 | tf_op jit(solution)/shard_map/gram/pallas_call | solution.py:459
  173.6 9.5 %gram.13 = (f32[40,128]{1,0:T(8,128)S(1)}, bf16[1024,5120]{1,0:T(8,128)(2,1)}) custom-call(bf16[640,1024]{1,0:T(8,128)(2,1)S(1)} %collective-permute-done.6.refs_0_, s32[40,128]{1,0:T(8,128)S(1)} %get-tuple-element.29.refs_1_, s32[5120,128]{1,0:T(8,128)S(1)} %get-tuple-element.30.refs_2_, ...), custom_call_target="tpu_custom_call", output_to_operand_aliasing={{1}: (4, {})} | custom-call | flops 1000 | bytes 1000 | tf_op jit(solution)/shard_map/gram/pallas_call | solution.py:459
  183.2 39.6 %reduce-scatter.5.cloned.1.call-done = f32[1,24,1024]{2,1,0:T(8,128)} async-done(((f32[8,24,1024]{2,1,0:T(8,128)}), f32[1,24,1024]{2,1,0:T(8,128)}) %reduce-scatter.5.cloned.1.call-update) | async-done | bytes 98320 | tf_op jit(solution)/shard_map/reduce_scatter | solution.py:608
  223.7 10.2 %all-gather = f32[128,1024]{1,0:T(8,128)S(1)} all-gather(f32[32,1024]{1,0:T(8,128)S(1)} %pack.1), channel_id=2, replica_groups=mesh['grp'=4,'docs'=8] {'grp'}, dimensions={0}, use_global_device_ids=true | all-gather | bytes 655360 | tf_op jit(solution)/shard_map/all_gather | solution.py:619
  234.8 10.6 %gram.14 = (f32[40,128]{1,0:T(8,128)S(1)}, bf16[1024,5120]{1,0:T(8,128)(2,1)}) custom-call(bf16[640,1024]{1,0:T(8,128)(2,1)} %collective-permute-done.5.refs_0_, s32[40,128]{1,0:T(8,128)S(1)} %get-tuple-element.29.refs_1_, s32[5120,128]{1,0:T(8,128)S(1)} %get-tuple-element.30.refs_2_, ...), custom_call_target="tpu_custom_call", output_to_operand_aliasing={{1}: (4, {})} | custom-call | flops 1000 | bytes 1000 | tf_op jit(solution)/shard_map/gram/pallas_call | solution.py:459
  245.4 13.0 %collective-permute-done.4.refs_0_ = bf16[640,1024]{1,0:T(8,128)(2,1)} collective-permute-done((bf16[640,1024]{1,0:T(8,128)(2,1)}, bf16[640,1024]{1,0:T(8,128)(2,1)}, u32[]{:S(2)}, u32[]{:S(2)}) %collective-permute-start.4) | collective-permute-done | bytes 1310752 | tf_op jit(solution)/shard_map/ppermute | solution.py:596
  258.4 13.1 %gram.15 = f32[8,16,128]{2,1,0:T(8,128)S(1)} custom-call(bf16[640,1024]{1,0:T(8,128)(2,1)} %collective-permute-done.4.refs_0_, s32[40,128]{1,0:T(8,128)S(1)} %get-tuple-element.29.refs_1_, s32[5120,128]{1,0:T(8,128)S(1)} %get-tuple-element.30.refs_2_, f32[40,128]{1,0:T(8,128)S(1)} %get-tuple-element.45.refs_3_, ...), custom_call_target="tpu_custom_call" | custom-call | flops 1000 | bytes 1000 | tf_op jit(solution)/shard_map/gram/pallas_call | solution.py:459
  271.5 10.2 %all_to_all.10.back_ref = f32[8,16,128]{2,1,0:T(8,128)S(1)} all-to-all(f32[8,16,128]{2,1,0:T(8,128)S(1)} %gram.15), channel_id=1, replica_groups=mesh['grp'=4,'docs'=8] {'docs'}, dimensions={0} | all-to-all | bytes 131072 | tf_op jit(solution)/shard_map/all_to_all | solution.py:626
  (48 shorter events, 18.1 us)
Async XLA Ops:
  7.2 101.2 %reduce-scatter.3.cloned.1.call-start = ((), (), s32[]{:S(2)}) async-start(), calls=%async_computation.4 | async-start | bytes 3932160 | tf_op jit(solution)/shard_map/reduce_scatter | solution.py:606
  7.2 0.7 copy-start.6
  7.9 0.7 copy-start.7
  14.5 34.7 %collective-permute-start.1 = (bf16[640,1024]{1,0:T(8,128)(2,1)S(1)}, bf16[640,1024]{1,0:T(8,128)(2,1)}, u32[]{:S(2)}, u32[]{:S(2)}) collective-permute-start(bf16[640,1024]{1,0:T(8,128)(2,1)S(1)} %unit.9.refs_0_.refs_1_), channel_id=1, source_target_pairs={{0,1},{1,2},{2,3},{3,4},{4,5},{5,6},{6,7},{7,0},{8,9},{9,10},{10,1... | collective-permute-start | bytes 3932168 | tf_op jit(solution)/shard_map/ppermute | solution.py:596
  15.0 34.4 %collective-permute-start = (bf16[640,1024]{1,0:T(8,128)(2,1)S(1)}, bf16[640,1024]{1,0:T(8,128)(2,1)}, u32[]{:S(2)}, u32[]{:S(2)}) collective-permute-start(bf16[640,1024]{1,0:T(8,128)(2,1)S(1)} %unit.8.refs_0_), channel_id=1, source_target_pairs={{0,2},{1,3},{2,4},{3,5},{4,6},{5,7},{6,0},{7,1},{8,10},{9,11},{10,... | collective-permute-start | bytes 3932168 | tf_op jit(solution)/shard_map/ppermute | solution.py:596
  20.1 13.9 %copy-start.2 = (bf16[640,1024]{1,0:T(8,128)(2,1)}, bf16[640,1024]{1,0:T(8,128)(2,1)S(1)}, u32[]{:S(2)}) copy-start(bf16[640,1024]{1,0:T(8,128)(2,1)S(1)} %unit.10.refs_0_.refs_2_) | copy-start | bytes 3932164
  49.4 58.0 %collective-permute-start.2 = (bf16[640,1024]{1,0:T(8,128)(2,1)}, bf16[640,1024]{1,0:T(8,128)(2,1)S(1)}, u32[]{:S(2)}, u32[]{:S(2)}) collective-permute-start(bf16[640,1024]{1,0:T(8,128)(2,1)} %copy-done.2), channel_id=1, source_target_pairs={{0,3},{1,4},{2,5},{3,6},{4,7},{5,0},{6,1},{7,2},{8,11},{9,12},{10,... | collective-permute-start | bytes 3932168 | tf_op jit(solution)/shard_map/ppermute | solution.py:596
  63.6 43.9 %all-to-all-start = ((s32[8,8,128]{2,1,0:T(8,128)}), s32[8,8,128]{2,1,0:T(8,128)S(1)}, u32[]{:S(2)}, u32[]{:S(2)}) async-start(s32[8,8,128]{2,1,0:T(8,128)} %hold.8), calls=%async_computation.1 | async-start | bytes 65536 | tf_op jit(solution)/shard_map/all_to_all | solution.py:604
  68.4 154.4 %reduce-scatter.5.cloned.1.call-start = ((), (), s32[]{:S(2)}) async-start(), calls=%async_computation.5 | async-start | bytes 884736 | tf_op jit(solution)/shard_map/reduce_scatter | solution.py:608
  107.4 4.1 %copy-start = (bf16[640,1024]{1,0:T(8,128)(2,1)}, bf16[640,1024]{1,0:T(8,128)(2,1)S(1)}, u32[]{:S(2)}) copy-start(bf16[640,1024]{1,0:T(8,128)(2,1)S(1)} %collective-permute-done.2.refs_1_.refs_0_) | copy-start | bytes 3932164
  107.5 33.6 %collective-permute-start.3 = (bf16[640,1024]{1,0:T(8,128)(2,1)S(1)}, bf16[640,1024]{1,0:T(8,128)(2,1)}, u32[]{:S(2)}, u32[]{:S(2)}) collective-permute-start(bf16[640,1024]{1,0:T(8,128)(2,1)S(1)} %hold.10), channel_id=1, source_target_pairs={{0,7},{1,0},{2,1},{3,2},{4,3},{5,4},{6,5},{7,6},{8,15},{9,8},{10,9... | collective-permute-start | bytes 3932168 | tf_op jit(solution)/shard_map/ppermute | solution.py:596
  108.3 1.1 copy-start.3
  109.5 0.9 copy-start.4
  110.4 63.2 %collective-permute-start.6 = (bf16[640,1024]{1,0:T(8,128)(2,1)}, bf16[640,1024]{1,0:T(8,128)(2,1)S(1)}, u32[]{:S(2)}, u32[]{:S(2)}) collective-permute-start(bf16[640,1024]{1,0:T(8,128)(2,1)} %hold.13), channel_id=1, source_target_pairs={{0,6},{1,7},{2,0},{3,1},{4,2},{5,3},{6,4},{7,5},{8,14},{9,15},{10,... | collective-permute-start | bytes 3932168 | tf_op jit(solution)/shard_map/ppermute | solution.py:596
  111.5 123.3 %collective-permute-start.5 = (bf16[640,1024]{1,0:T(8,128)(2,1)}, bf16[640,1024]{1,0:T(8,128)(2,1)}, u32[]{:S(2)}, u32[]{:S(2)}) collective-permute-start(bf16[640,1024]{1,0:T(8,128)(2,1)} %hold.12), channel_id=1, source_target_pairs={{0,5},{1,6},{2,7},{3,0},{4,1},{5,2},{6,3},{7,4},{8,13},{9,14},{10,... | collective-permute-start | bytes 3932168 | tf_op jit(solution)/shard_map/ppermute | solution.py:596
  141.0 117.4 %collective-permute-start.4 = (bf16[640,1024]{1,0:T(8,128)(2,1)}, bf16[640,1024]{1,0:T(8,128)(2,1)}, u32[]{:S(2)}, u32[]{:S(2)}) collective-permute-start(bf16[640,1024]{1,0:T(8,128)(2,1)} %hold.11), channel_id=1, source_target_pairs={{0,4},{1,5},{2,6},{3,7},{4,0},{5,1},{6,2},{7,3},{8,12},{9,13},{10,... | collective-permute-start | bytes 3932168 | tf_op jit(solution)/shard_map/ppermute | solution.py:596
  152.3 6.4 %copy-start.1 = (bf16[640,1024]{1,0:T(8,128)(2,1)S(1)}, bf16[640,1024]{1,0:T(8,128)(2,1)}, u32[]{:S(2)}) copy-start(bf16[640,1024]{1,0:T(8,128)(2,1)} %copy-done) | copy-start | bytes 3932164
  222.8 0.9 copy-start.5
Sparse Core Ops, SparseCore 0:
  49.5 56.4 reduce-scatter.2
  110.5 112.2 reduce-scatter.4
